TPU v7x, 128 devices: a whole 4x4x4 slice. The times are simulated.
128 devices in a mesh: rep: 2 (over y_hi), shard: 64 (over x, y_lo, z, core).
Axes of the slice: x: 4, y: 4 (y_hi: 2, y_lo: 2; y = y_hi * 2 + y_lo), z: 4, core: 2. Of those that a mesh axis runs over, the one named last changes fastest.
Arguments:
- layer_in: bfloat16 [2, 2, 4096, 2048], P(None, 'rep', 'shard'), may hold values from -6 to 6
- cotangent: bfloat16 [2, 2, 4096, 2048], P(None, 'rep', 'shard'), may hold values from -6 to 6
- segment_ids: int32 [2, 2, 4096], P(None, 'rep', 'shard'), may hold values from 0 to 4095, as said below
- norm_gain: float32 [2048], P('shard'), may hold values from 0.5 to 1.5
- in_weight: bfloat16 [2048, 8512], P('shard'), may hold values from -0.125 to 0.125
- conv_weight: float32 [4, 4352], P(None, 'shard'), may hold values from -3 to 3
- conv_bias: float32 [4352], P('shard'), may hold values from -0.5 to 0.5
- dt_bias: float32 [64], P('shard'), may hold values from -7 to -5
- a_log: float32 [64], P('shard')
- skip_gain: float32 [64], P('shard'), may hold values from 0.5 to 1.5
- out_gain: float32 [4096], P('shard'), may hold values from 0.5 to 1.5
- out_weight: bfloat16 [4096, 2048], P('shard'), may hold values from -0.09375 to 0.09375
Outputs:
- layer_out: bfloat16 [2, 2, 4096, 2048], P(None, 'rep', 'shard')
- grad_layer_in: bfloat16 [2, 2, 4096, 2048], P(None, 'rep', 'shard')
- grad_norm_gain: float32 [2048], P('shard')
- grad_in_weight: float32 [2048, 8512], P('shard')
- grad_conv_weight: float32 [4, 4352], P(None, 'shard')
- grad_conv_bias: float32 [4352], P('shard')
- grad_dt_bias: float32 [64], P('shard')
- grad_a_log: float32 [64], P('shard')
- grad_skip_gain: float32 [64], P('shard')
- grad_out_gain: float32 [4096], P('shard')
- grad_out_weight: float32 [4096, 2048], P('shard')
Inputs may be any that keep to these rules, and one draw needn't show every extreme that they name: `segment_ids`: along each sequence the numbers never fall and start at 0; they rise by at most 1 from one token to the next, except that the last token of every sequence is a document of its own numbered 4096 - 1. In each sequence position of the 2 micro-batches, one micro-batch holds a document that begins within the first 64 tokens and ends within the last 64.
All inputs are finite; a program needn't handle non-finite values.
Results may differ from a plain program's by a relative error of at most 0.0066.
Values may be sent and summed in bfloat16 or wider, within the bound.
A program may use at most 768 MiB of HBM per device.

v0:
```python
from functools import partial

import jax
import jax.numpy as jnp
from jax import lax
from jax.sharding import PartitionSpec as P

INNER = 4096
NH = 64
HEADDIM = 64
STATE = 128
MICRO = 2
CONV = 4352


EPS = 1e-05
HIGH = lax.Precision.HIGHEST


def from_behind(value, axis, steps):
    count = lax.axis_size(axis)
    leading, last = (max(0, -steps), min(count, count - steps))
    return lax.ppermute(value, axis, [(source, source + steps) for source in range(leading, last)])


def entering(value, axis, combine, identity, reverse):
    size, mine = (lax.axis_size(axis), lax.axis_index(axis))
    everything = jax.tree.map(lambda part: lax.all_gather(part, axis), value)
    start = jax.tree.map(
        lambda part, zero: jnp.broadcast_to(jnp.asarray(zero, part.dtype), part.shape),
        value,
        identity,
    )

    def hop(k, before):
        at = size - 1 - k if reverse else k
        reached = at > mine if reverse else at < mine
        new = combine(before, jax.tree.map(lambda part: part[at], everything))
        return jax.tree.map(lambda a, b: jnp.where(reached, a, b), new, before)

    return lax.fori_loop(0, size, hop, start)


def rms_scale(values, gain):
    return values * lax.rsqrt(jnp.mean(values * values, axis=-1, keepdims=True) + EPS) * gain


def link_states(earlier, later):
    return (earlier[0] * later[0], later[0][:, None, None] * earlier[1] + later[1])


def conv_front(ext_rows, dt_raw, conv_full, cbias_full, dtb_full, alog_full, tap_masks):
    count = dt_raw.shape[0]
    total = jnp.zeros((count, cbias_full.shape[0]), jnp.float32) + cbias_full[None, :]
    for tap in range(4):
        total = (
            total + conv_full[tap][None, :] * ext_rows[tap : tap + count] * tap_masks[tap][:, None]
        )
    acts = jax.nn.silu(total)
    inputs = acts[:, :INNER].reshape(count, NH, HEADDIM)
    b_rows = acts[:, INNER : INNER + STATE]
    c_rows = acts[:, INNER + STATE :]
    delta = jax.nn.softplus(dt_raw + dtb_full[None, :])
    cumul = jnp.cumsum(delta * (-jnp.exp(alog_full))[None, :], axis=0)
    return (inputs, b_rows, c_rows, delta, cumul)


def block_state(inputs, b_rows, delta, cumul, to_end, ends_joined):
    count = delta.shape[0]
    weight_end = jnp.exp(cumul[count - 1][None, :] - cumul) * to_end[:, None]
    driven = delta[:, :, None] * inputs
    local_state = jnp.einsum("sh,shp,sn->hpn", weight_end, driven, b_rows, precision=HIGH)
    return (jnp.exp(cumul[count - 1]) * ends_joined, local_state)


def block_output(
    inputs,
    b_rows,
    c_rows,
    delta,
    cumul,
    state_in,
    gate_part,
    skip_full,
    ogain_full,
    same_causal,
    carry_on,
):
    count = delta.shape[0]
    keep = same_causal[:, :, None]
    spread = jnp.where(
        keep, jnp.exp(jnp.where(keep, cumul[:, None, :] - cumul[None, :, :], 0.0)), 0.0
    )
    scores = jnp.einsum("tn,sn->ts", c_rows, b_rows, precision=HIGH)
    driven = delta[:, :, None] * inputs
    inner_part = jnp.einsum("tsh,shp->thp", scores[:, :, None] * spread, driven, precision=HIGH)
    carried = (
        jnp.einsum("tn,hpn->thp", c_rows, state_in, precision=HIGH)
        * (jnp.exp(cumul) * carry_on[:, None])[:, :, None]
    )
    mixed = inner_part + carried + skip_full[None, :, None] * inputs
    gated = mixed.reshape(count, INNER) * jax.nn.silu(gate_part)
    return rms_scale(gated, ogain_full)


def weight_terms(normed_rows, proj_grads, out_rows, cot_rows):
    left = out_rows
    out_grad = lax.psum_scatter(
        jnp.einsum("tn,tj->nj", left, cot_rows, preferred_element_type=jnp.float32),
        "shard",
        scatter_dimension=0,
        tiled=True,
    )
    left = normed_rows
    in_grad = lax.psum_scatter(
        jnp.einsum("tn,tj->nj", left, proj_grads, preferred_element_type=jnp.float32),
        "shard",
        scatter_dimension=0,
        tiled=True,
    )
    return (in_grad, out_grad)


def per_device(
    layer_in,
    cotangent,
    segment_ids,
    norm_gain,
    in_weight,
    conv_weight,
    conv_bias,
    dt_bias,
    a_log,
    skip_gain,
    out_gain,
    out_weight,
):
    norm_full, conv_full, cbias_full, dtb_full, alog_full, skip_full, ogain_full = (
        lax.all_gather(norm_gain, "shard", axis=0, tiled=True),
        lax.all_gather(conv_weight, "shard", axis=1, tiled=True),
        lax.all_gather(conv_bias, "shard", axis=0, tiled=True),
        lax.all_gather(dt_bias, "shard", axis=0, tiled=True),
        lax.all_gather(a_log, "shard", axis=0, tiled=True),
        lax.all_gather(skip_gain, "shard", axis=0, tiled=True),
        lax.all_gather(out_gain, "shard", axis=0, tiled=True),
    )
    in_full, out_full = (
        lax.all_gather(in_weight, "shard", axis=0, tiled=True),
        lax.all_gather(out_weight, "shard", axis=0, tiled=True),
    )
    count = layer_in.shape[2]
    positions = jnp.arange(count)
    lower = positions[:, None] >= positions[None, :]
    scan_start = (jnp.ones((NH,), jnp.float32), jnp.zeros((NH, HEADDIM, STATE), jnp.float32))
    saved = []
    outputs = []
    for index in range(MICRO):
        hidden = layer_in[index, 0].astype(jnp.float32)
        seg_ids = segment_ids[index, 0]
        own_mod = (seg_ids % 64).astype(jnp.bfloat16)
        normed_f, norm_back = jax.vjp(rms_scale, hidden, norm_full)
        normed_b = normed_f.astype(jnp.bfloat16)
        proj = jnp.dot(normed_b, in_full, preferred_element_type=jnp.float32)
        gate_part = proj[:, :INNER]
        xbc_b = proj[:, INNER : INNER + CONV].astype(jnp.bfloat16)
        dt_raw = proj[:, INNER + CONV :]
        prev_rows, prev_mod = from_behind((xbc_b[count - 3 :], own_mod[count - 3 :]), "shard", 1)
        own_f = own_mod.astype(jnp.float32)
        prev_f = prev_mod.astype(jnp.float32)
        ext_mod = jnp.concatenate([prev_f, own_f])
        ext_int = jnp.concatenate([jnp.full((3,), -1, jnp.int32), seg_ids])
        mask_list = []
        for tap in range(4):
            within = ext_int[tap : tap + count] == seg_ids
            across = ext_mod[tap : tap + count] == own_f
            mask_list.append(
                jnp.where(positions - 3 + tap >= 0, within, across).astype(jnp.float32)
            )
        tap_masks = jnp.stack(mask_list)
        first_joined = (own_f[0] == prev_f[2]).astype(jnp.float32)
        carry_on = (seg_ids == seg_ids[0]).astype(jnp.float32) * first_joined
        to_end = (seg_ids == seg_ids[count - 1]).astype(jnp.float32)
        ends_joined = to_end[0] * first_joined
        same_causal = (seg_ids[:, None] == seg_ids[None, :]) & lower
        ext_rows = jnp.concatenate([prev_rows, xbc_b], 0).astype(jnp.float32)
        front, front_back = jax.vjp(
            partial(conv_front, tap_masks=tap_masks),
            ext_rows,
            dt_raw,
            conv_full,
            cbias_full,
            dtb_full,
            alog_full,
        )
        inputs, b_rows, c_rows, delta, cumul = front
        block_end, state_back = jax.vjp(
            partial(block_state, to_end=to_end, ends_joined=ends_joined),
            inputs,
            b_rows,
            delta,
            cumul,
        )
        carried_in = entering(block_end, "shard", link_states, scan_start, False)
        state_in = carried_in[1]
        normed_out, out_back = jax.vjp(
            partial(block_output, same_causal=same_causal, carry_on=carry_on),
            inputs,
            b_rows,
            c_rows,
            delta,
            cumul,
            state_in,
            gate_part,
            skip_full,
            ogain_full,
        )
        normed_out_b = normed_out.astype(jnp.bfloat16)
        branch = jnp.dot(normed_out_b, out_full, preferred_element_type=jnp.float32)
        outputs.append((hidden + branch).astype(jnp.bfloat16))
        saved.append(
            (
                norm_back,
                normed_b,
                front_back,
                state_back,
                out_back,
                block_end,
                state_in,
                normed_out_b,
            )
        )
    in_back, out_back_rows = (in_full, out_full)
    small_sums = None
    big_sums = None
    kept_rows = []
    input_grads = []
    for index in range(MICRO):
        norm_back, normed_b, front_back, state_back, out_back, block_end, state_in, normed_out_b = (
            saved[index]
        )
        cot_rows = cotangent[index, 0]
        d_normed_out = jnp.einsum(
            "td,nd->tn", cot_rows, out_back_rows, preferred_element_type=jnp.float32
        )
        d_inputs, d_brows, d_crows, d_delta, d_cumul, d_state_in, d_gate, d_skip, d_ogain = (
            out_back(d_normed_out)
        )
        later_in = entering((block_end[0], d_state_in), "shard", link_states, scan_start, True)
        grad_end = later_in[1]
        d_decay = jnp.sum(grad_end * state_in, axis=(1, 2))
        s_inputs, s_brows, s_delta, s_cumul = state_back((d_decay, grad_end))
        d_ext, d_dt_raw, d_conv, d_cbias, d_dtb, d_alog = front_back(
            (d_inputs + s_inputs, d_brows + s_brows, d_crows, d_delta + s_delta, d_cumul + s_cumul)
        )
        from_next = from_behind(d_ext[:3].astype(jnp.bfloat16), "shard", -1).astype(jnp.float32)
        d_xbc = d_ext[3:] + jnp.concatenate(
            [jnp.zeros((count - 3, CONV), jnp.float32), from_next], 0
        )
        d_proj = jnp.concatenate([d_gate, d_xbc, d_dt_raw], 1).astype(jnp.bfloat16)
        d_normed = jnp.einsum("tj,nj->tn", d_proj, in_back, preferred_element_type=jnp.float32)
        d_hidden, d_norm = norm_back(d_normed)
        input_grads.append((cot_rows.astype(jnp.float32) + d_hidden).astype(jnp.bfloat16))
        small_terms = (d_norm, d_conv, d_cbias, d_dtb, d_alog, d_skip, d_ogain)
        small_sums = (
            small_terms if small_sums is None else jax.tree.map(jnp.add, small_sums, small_terms)
        )
        kept_rows.append((normed_b, d_proj, normed_out_b, cot_rows))
    big_sums = weight_terms(
        jnp.concatenate([item[0] for item in kept_rows], 0),
        jnp.concatenate([item[1] for item in kept_rows], 0),
        jnp.concatenate([item[2] for item in kept_rows], 0),
        jnp.concatenate([item[3] for item in kept_rows], 0),
    )
    d_small = (
        lax.psum_scatter(small_sums[0], "shard", scatter_dimension=0, tiled=True),
        lax.psum_scatter(small_sums[1], "shard", scatter_dimension=1, tiled=True),
        lax.psum_scatter(small_sums[2], "shard", scatter_dimension=0, tiled=True),
        lax.psum_scatter(small_sums[3], "shard", scatter_dimension=0, tiled=True),
        lax.psum_scatter(small_sums[4], "shard", scatter_dimension=0, tiled=True),
        lax.psum_scatter(small_sums[5], "shard", scatter_dimension=0, tiled=True),
        lax.psum_scatter(small_sums[6], "shard", scatter_dimension=0, tiled=True),
    )
    totals = lax.psum(
        (
            d_small[0],
            big_sums[0],
            d_small[1],
            d_small[2],
            d_small[3],
            d_small[4],
            d_small[5],
            d_small[6],
            big_sums[1],
        ),
        "rep",
    )
    layer_out = jnp.stack(outputs)[:, None]
    grad_layer_in = jnp.stack(input_grads)[:, None]
    return (
        layer_out,
        grad_layer_in,
        totals[0],
        totals[1],
        totals[2],
        totals[3],
        totals[4],
        totals[5],
        totals[6],
        totals[7],
        totals[8],
    )


def solution(mesh):
    return jax.shard_map(
        per_device,
        mesh=mesh,
        in_specs=(
            P(None, "rep", "shard", None),
            P(None, "rep", "shard", None),
            P(None, "rep", "shard"),
            P("shard"),
            P("shard", None),
            P(None, "shard"),
            P("shard"),
            P("shard"),
            P("shard"),
            P("shard"),
            P("shard"),
            P("shard", None),
        ),
        out_specs=(
            P(None, "rep", "shard", None),
            P(None, "rep", "shard", None),
            P("shard"),
            P("shard", None),
            P(None, "shard"),
            P("shard"),
            P("shard"),
            P("shard"),
            P("shard"),
            P("shard"),
            P("shard", None),
        ),
        check_vma=False,
    )
```

profile of v0, /device:TPU:1, one launch (start us, length us, event | category | flops | bytes accessed | tf_op | source)
XLA Modules:
  0.0 4873.9 jit_solution(86545873449613248)
XLA Ops:
  9.5 4.9 collective-permute-start.1
  22.7 83.0 %all-gather.4 = f32[64,68,4]{1,2,0:T(4,128)S(1)} all-gather(f32[1,68,4]{1,2,0:T(4,128)} %bitcast.296), channel_id=1, replica_groups=mesh['rep'=2,'shard'=64] {'shard'}, dimensions={0}, use_global_device_ids=true | all-gather | bytes 70720 | tf_op jit(solution)/shard_map/all_gather | solution.py:140
  110.7 270.8 %all-reduce.44 = (f32[2048]{0:T(1024)S(1)}, f32[4352]{0:T(1024)S(1)}, f32[64]{0:T(128)S(1)}, f32[64]{0:T(128)S(1)}, f32[64]{0:T(128)}, /*index=5*/f32[4096]{0:T(1024)}) all-reduce(f32[2048]{0:T(1024)S(1)} %dynamic-update-slice, f32[4352]{0:T(1024)S(1)} %dynamic-update-slice.2, ...), channel_id=1, replica_groups=mesh['rep'=2,'shard'=64] {'shard'}, use_global_device_ids=true, to_apply=%add.30 | all-reduce | flops 10688 | bytes 85504
  391.1 14.2 fusion.274
  406.2 14.2 fusion.275
  450.9 12.3 fusion.257
  467.5 83.3 %all-gather.6 = f32[64,1,64]{2,1,0:T(1,128)} all-gather(f32[1,1,64]{2,1,0:T(1,128)} %get-tuple-element.751), channel_id=1, replica_groups=mesh['rep'=2,'shard'=64] {'shard'}, dimensions={0}, use_global_device_ids=true | all-gather | bytes 16640 | tf_op jit(solution)/shard_map/all_gather | solution.py:28
  550.8 78.1 %all-gather.5 = f32[64,1,64]{2,1,0:T(1,128)} all-gather(f32[1,1,64]{2,1,0:T(1,128)} %get-tuple-element.747), channel_id=1, replica_groups=mesh['rep'=2,'shard'=64] {'shard'}, dimensions={0}, use_global_device_ids=true | all-gather | bytes 16640 | tf_op jit(solution)/shard_map/all_gather | solution.py:28
  632.0 519.4 %all-gather.20.cloned.1.call-done = f32[4096,64,128]{2,1,0:T(8,128)} async-done(((f32[64,64,128]{2,1,0:T(8,128)}), f32[4096,64,128]{2,1,0:T(8,128)}) %all-gather.20.cloned.1.call-update) | async-done | bytes 134217744 | tf_op jit(solution)/shard_map/all_gather | solution.py:28
  1151.4 331.0 %while.61 = (s32[]{:T(128)}, f32[64,64,128]{2,1,0:T(8,128)}, s32[]{:T(128)}, f32[64,64]{1,0:T(8,128)}, f32[64,64,64,128]{3,2,1,0:T(8,128)}, /*index=5*/s32[]{:T(128)}, s32[]{:T(128)}) while((s32[]{:T(128)}, f32[64,64,128]{2,1,0:T(8,128)}, s32[]{:T(128)}, f32[64,64]{1,0:T(8,128)}, f32[64,64,64,128]{3,2,1,0:T(8,128)}, ...), condition=%wide.region_8.10_spmd.clone, body=%wide.region_7.9_spmd.clone.sunk | while | flops 2097156 | bytes 6292337 | solution.py:41
  1162.1 4.8 fusion.305
  1203.9 4.1 fusion.305
  1400.5 4.1 fusion.305
  1486.1 5.2 fusion.42
  1498.1 365.6 %all-gather.18.cloned.1.call-done = f32[4096,64,128]{2,1,0:T(8,128)} async-done(((f32[64,64,128]{2,1,0:T(8,128)}), f32[4096,64,128]{2,1,0:T(8,128)}) %all-gather.18.cloned.1.call-update) | async-done | bytes 134217744 | tf_op jit(solution)/shard_map/all_gather | solution.py:28
  1863.6 210.8 %while.60 = (s32[]{:T(128)}, f32[64,64,128]{2,1,0:T(8,128)S(1)}, s32[]{:T(128)}, f32[64,64]{1,0:T(8,128)}, f32[64,64,64,128]{3,2,1,0:T(8,128)}, /*index=5*/s32[]{:T(128)}, s32[]{:T(128)}) while((s32[]{:T(128)}, f32[64,64,128]{2,1,0:T(8,128)S(1)}, s32[]{:T(128)}, f32[64,64]{1,0:T(8,128)}, f32[64,64,64,128]{3,2,1,0:T(8,128)}, ...), condition=%wide.region_3.5_spmd.clone, body=%wide.region_2.4_spmd.clone.sunk | while | flops 2097156 | bytes 6292337 | solution.py:41
  2077.3 5.4 fusion.43
  2089.8 13.7 multiply_reduce_fusion.17
  2104.9 6.8 multiply_reduce_fusion.18
  2118.2 4.7 fusion.54
  2129.4 4.7 fusion.58
  2136.5 7.4 fusion.89
  2151.8 7.6 fusion.87
  2167.4 6.3 fusion.107
  2188.6 13.7 fusion.128
  2202.3 631.6 %all-gather.24.cloned.1.call-done = f32[4096,64,128]{2,1,0:T(8,128)} async-done(((f32[64,64,128]{2,1,0:T(8,128)}), f32[4096,64,128]{2,1,0:T(8,128)}) %all-gather.24.cloned.1.call-update) | async-done | bytes 134217744 | tf_op jit(solution)/shard_map/all_gather | solution.py:28
  2833.9 297.7 %while.63 = (s32[]{:T(128)}, f32[64,64,128]{2,1,0:T(8,128)}, s32[]{:T(128)}, f32[64,64]{1,0:T(8,128)}, f32[64,64,64,128]{3,2,1,0:T(8,128)}, /*index=5*/s32[]{:T(128)}, s32[]{:T(128)}, s32[]{:T(128)}, s32[]{:T(128)}) while((s32[]{:T(128)}, f32[64,64,128]{2,1,0:T(8,128)}, s32[]{:T(128)}, f32[64,64]{1,0:T(8,128)}, ...), condition=%wide.region_26.28_spmd.clone, body=%wide.region_25.27_spmd.clone.sunk | while | flops 2097160 | bytes 6292399 | solution.py:41
  2875.5 4.1 fusion.307
  2903.5 4.2 fusion.307
  2931.5 4.1 fusion.307
  2959.6 4.1 fusion.307
  2987.6 4.1 fusion.307
  3015.7 4.1 fusion.307
  3131.7 8.5 multiply_reduce_fusion.4
  3144.5 401.9 %all-gather.22.cloned.1.call-done = f32[4096,64,128]{2,1,0:T(8,128)} async-done(((f32[64,64,128]{2,1,0:T(8,128)}), f32[4096,64,128]{2,1,0:T(8,128)}) %all-gather.22.cloned.1.call-update) | async-done | bytes 134217744 | tf_op jit(solution)/shard_map/all_gather | solution.py:28
  3546.4 293.6 %while.62 = (s32[]{:T(128)}, f32[64,64,128]{2,1,0:T(8,128)}, s32[]{:T(128)}, f32[64,64]{1,0:T(8,128)}, f32[64,64,64,128]{3,2,1,0:T(8,128)}, /*index=5*/s32[]{:T(128)}, s32[]{:T(128)}, s32[]{:T(128)}, s32[]{:T(128)}) while((s32[]{:T(128)}, f32[64,64,128]{2,1,0:T(8,128)}, s32[]{:T(128)}, f32[64,64]{1,0:T(8,128)}, ...), condition=%wide.region_13.15_spmd.clone, body=%wide.region_12.14_spmd.clone.sunk | while | flops 2097160 | bytes 6292399 | solution.py:41
  3840.0 8.5 multiply_reduce_fusion.7
  3859.3 6.0 fusion.101
  3889.2 27.2 fusion.8
  3919.7 8.9 fusion.6
  3928.6 9.1 fusion.7
  3939.7 16.6 fusion.116
  3956.3 369.6 %reduce-scatter.4.cloned.1.call-done = f32[32,8512]{1,0:T(8,128)} async-done(((f32[2048,8512]{1,0:T(8,128)}), f32[32,8512]{1,0:T(8,128)}) %reduce-scatter.4.cloned.1.call-update) | async-done | bytes 1089552 | tf_op jit(solution)/shard_map/reduce_scatter | solution.py:115
  4326.0 16.6 fusion.177
  4342.6 276.4 %all-reduce.43 = (f32[2048]{0:T(1024)S(1)}, f32[4352]{0:T(1024)S(1)}, f32[64]{0:T(128)S(1)}, f32[64]{0:T(128)S(1)}, f32[64]{0:T(128)S(1)}, /*index=5*/f32[4096]{0:T(1024)S(1)}) all-reduce(f32[2048]{0:T(1024)S(1)} %add.510, f32[4352]{0:T(1024)S(1)} %add.512, f32[64]{0:T(128)S(1)} %add.513, ...), channel_id=6, replica_groups=mesh['rep'=2,'shard'=64] {'shard'}, use_global_device_ids=true, to_apply=%region_38.40.clone | all-reduce | flops 10688 | bytes 85504
  4624.1 177.4 %all-reduce.50.cloned.1.call-done = f32[4,4352]{1,0:T(4,128)} async-done(((f32[4,4352]{1,0:T(4,128)}), f32[4,4352]{1,0:T(4,128)}) %all-reduce.50.cloned.1.call-update) | async-done | bytes 69648
  4802.3 6.0 all-reduce.45
  4808.3 55.4 %all-reduce.52.cloned.1.call-done = (f32[32,8512]{1,0:T(8,128)}, f32[64,2048]{1,0:T(8,128)}) async-done(((f32[32,8512]{1,0:T(8,128)}, f32[64,2048]{1,0:T(8,128)}), (f32[32,8512]{1,0:T(8,128)}, f32[64,2048]{1,0:T(8,128)})) %all-reduce.52.cloned.1.call-update) | async-done | bytes 1613840 | tf_op jit(solution)/shard_map/psum | solution.py:283
  (982 shorter events, 1267.8 us)
Async XLA Ops:
  7.2 376.7 %copy-start.93 = (s32[2,1,64]{2,1,0:T(1,128)S(1)}, s32[2,1,64]{2,1,0:T(1,128)}, u32[]{:S(2)}) copy-start(s32[2,1,64]{2,1,0:T(1,128)} %param.23) | copy-start | bytes 1540
  7.2 375.9 %copy-start.14 = (bf16[2,1,64,2048]{3,2,1,0:T(8,128)(2,1)S(1)}, bf16[2,1,64,2048]{3,2,1,0:T(8,128)(2,1)}, u32[]{:S(2)}) copy-start(bf16[2,1,64,2048]{3,2,1,0:T(8,128)(2,1)} %param.21) | copy-start | bytes 1572868
  7.2 383.8 %all-gather.14.cloned.1.call-start = ((), (), s32[]{:S(2)}) async-start(), calls=%async_computation.2 | async-start | bytes 35676160 | tf_op jit(solution)/shard_map/all_gather | solution.py:148
  7.9 443.0 %all-gather.16.cloned.1.call-start = ((), (), s32[]{:S(2)}) async-start(), calls=%async_computation.3 | async-start | bytes 17039360 | tf_op jit(solution)/shard_map/all_gather | solution.py:149
  8.7 1142.7 %all-gather.20.cloned.1.call-start = ((), (), s32[]{:S(2)}) async-start(), calls=%async_computation.7 | async-start | bytes 136314880 | tf_op jit(solution)/shard_map/all_gather | solution.py:28
  9.5 375.9 %collective-permute-start.1 = (bf16[3]{0:T(256)(128)(2,1)S(1)}, bf16[3]{0:T(256)(128)(2,1)S(1)}, u32[]{:S(2)}, u32[]{:S(2)}) collective-permute-start(bf16[3]{0:T(256)(128)(2,1)S(1)} %slice.214), channel_id=1, source_target_pairs={{0,1},{1,2},{2,3},{3,4},{4,5},{5,6},{6,7},{7,8},{8,9},{9,10},{10,1... | collective-permute-start | bytes 26 | tf_op jit(solution)/shard_map/ppermute | solution.py:23
  14.5 372.9 %collective-permute-start.3 = (bf16[3]{0:T(256)(128)(2,1)S(1)}, bf16[3]{0:T(256)(128)(2,1)S(1)}, u32[]{:S(2)}, u32[]{:S(2)}) collective-permute-start(bf16[3]{0:T(256)(128)(2,1)S(1)} %slice.243), channel_id=1, source_target_pairs={{0,1},{1,2},{2,3},{3,4},{4,5},{5,6},{6,7},{7,8},{8,9},{9,10},{10,1... | collective-permute-start | bytes 26 | tf_op jit(solution)/shard_map/ppermute | solution.py:23
  381.5 23.7 copy-start.136
  381.5 44.6 copy-start.125
  383.1 47.3 copy-start.54
  383.1 47.3 copy-start.56
  383.1 47.3 copy-start.58
  383.1 47.3 copy-start.60
  383.8 42.3 copy-start.127
  385.2 42.3 copy-start.98
  385.2 56.4 %copy-start.96 = (f32[64]{0:T(128)}, f32[64]{0:T(128)S(1)}, u32[]{:S(2)}) copy-start(f32[64]{0:T(128)S(1)} %get-tuple-element.775) | copy-start | bytes 772
  385.4 19.9 copy-start.34
  385.4 20.8 copy-start.36
  390.8 36.7 copy-start.123
  390.8 50.8 %copy-start.121 = (f32[64]{0:T(128)}, f32[64]{0:T(128)S(1)}, u32[]{:S(2)}) copy-start(f32[64]{0:T(128)S(1)} %get-tuple-element.767) | copy-start | bytes 772
  390.9 39.5 copy-start.104
  390.9 39.5 copy-start.106
  390.9 39.5 copy-start.108
  391.0 39.5 copy-start.110
  391.0 39.5 copy-start.112
  391.0 39.5 copy-start.114
  405.3 20.9 copy-start.16
  420.5 8.4 collective-permute-start
  424.0 6.2 collective-permute-start.2
  440.9 1422.8 %all-gather.18.cloned.1.call-start = ((), (), s32[]{:S(2)}) async-start(), calls=%async_computation.6 | async-start | bytes 136314880 | tf_op jit(solution)/shard_map/all_gather | solution.py:28
  449.3 2384.6 %all-gather.24.cloned.1.call-start = ((), (), s32[]{:S(2)}) async-start(), calls=%async_computation.9 | async-start | bytes 136314880 | tf_op jit(solution)/shard_map/all_gather | solution.py:28
  2122.9 1423.5 %all-gather.22.cloned.1.call-start = ((), (), s32[]{:S(2)}) async-start(), calls=%async_computation.8 | async-start | bytes 136314880 | tf_op jit(solution)/shard_map/all_gather | solution.py:28
  2134.1 1822.1 %reduce-scatter.6.cloned.1.call-start = ((), (), s32[]{:S(2)}) async-start(), calls=%async_computation.5 | async-start | bytes 34078720 | tf_op jit(solution)/shard_map/reduce_scatter | solution.py:108
  2202.3 2123.6 %reduce-scatter.4.cloned.1.call-start = ((), (), s32[]{:S(2)}) async-start(), calls=%async_computation.4 | async-start | bytes 71352320 | tf_op jit(solution)/shard_map/reduce_scatter | solution.py:115
  2833.9 297.8 %copy-start.131 = (f32[64]{0:T(128)S(1)}, f32[64]{0:T(128)}, u32[]{:S(2)}) copy-start(f32[64]{0:T(128)} %get-tuple-element.679) | copy-start | bytes 772
  3876.3 10.0 collective-permute-start.5
  3878.9 8.8 collective-permute-start.4
  3916.4 885.1 %all-reduce.50.cloned.1.call-start = ((), (), s32[]{:S(2)}) async-start(), calls=%async_computation.10 | async-start | bytes 139264
  3928.6 10.2 copy-start.137
  3928.6 11.0 copy-start.26
  3939.6 386.3 %copy-start.87 = (f32[2048]{0:T(1024)S(1)}, f32[2048]{0:T(1024)}, u32[]{:S(2)}) copy-start(f32[2048]{0:T(1024)} %copy-done.86) | copy-start | bytes 24580
  3939.6 386.3 %copy-start.118 = (f32[64]{0:T(128)S(1)}, f32[64]{0:T(128)}, u32[]{:S(2)}) copy-start(f32[64]{0:T(128)} %copy-done.117) | copy-start | bytes 772
  3939.6 386.3 %copy-start.120 = (f32[64]{0:T(128)S(1)}, f32[64]{0:T(128)}, u32[]{:S(2)}) copy-start(f32[64]{0:T(128)} %copy-done.119) | copy-start | bytes 772
  3939.6 924.1 %all-reduce.52.cloned.1.call-start = ((), (), s32[]{:S(2)}) async-start(), calls=%async_computation.11 | async-start | bytes 3244032 | tf_op jit(solution)/shard_map/psum | solution.py:283
  4325.9 16.6 copy-start.92
  4326.0 296.9 %copy-start.133 = (f32[64]{0:T(128)S(1)}, f32[64]{0:T(128)}, u32[]{:S(2)}) copy-start(f32[64]{0:T(128)} %copy-done.132) | copy-start | bytes 772
  4326.0 296.9 %copy-start.135 = (f32[64]{0:T(128)S(1)}, f32[64]{0:T(128)}, u32[]{:S(2)}) copy-start(f32[64]{0:T(128)} %copy-done.134) | copy-start | bytes 772
  4326.0 296.9 %copy-start.27 = (bf16[2,1,64,2048]{3,2,1,0:T(8,128)(2,1)S(1)}, bf16[2,1,64,2048]{3,2,1,0:T(8,128)(2,1)}, u32[]{:S(2)}) copy-start(bf16[2,1,64,2048]{3,2,1,0:T(8,128)(2,1)} %param.22) | copy-start | bytes 1572868
  (108 other events, 407.3 us)
Sparse Core Ops, SparseCore 0:
  9.7 200.7 all-gather.13
  212.3 123.6 all-gather.15
  441.0 710.3 all-gather.19
  1153.0 710.5 all-gather.17
  2123.0 710.8 all-gather.23
  2835.5 710.8 all-gather.21
  3548.8 336.3 reduce-scatter.5
  3916.5 409.3 reduce-scatter.3
  4329.1 472.4 all-reduce.49
  4803.9 59.7 all-reduce.51
where the time goes:
time: 4900 us; the launch traced here: 4870 us
  waiting for transfers between devices  2520 us (51%)
  other arithmetic  943 us (19%)
  blocking collectives  798 us (16%)
  local copies, waits for them, and re-layouts  317 us (6%)
  matrix products  248 us (5%)
    all_gather x4, waiting for transfers between devices, entering(): everything = jax.tree.map(lambda part: lax.all_gather(part, axis), value)  1920 us
    select_n x256, other arithmetic, hop(): return jax.tree.map(lambda a, b: jnp.where(reached, a, b), new, before)  891 us
    unnamed x2, blocking collectives  547 us
    reduce_scatter x1, waiting for transfers between devices, weight_terms(): lax.psum_scatter(jnp.einsum('tn,tj->nj', left, proj_grads, preferred_elem...  370 us
    mul x256, local copies, waits for them, and re-layouts, link_states(): later[0][:, None, None] * earlier[1] + later[1]  240 us
    unnamed x11, waiting for transfers between devices  179 us
    all_gather x2, blocking collectives, entering(): everything = jax.tree.map(lambda part: lax.all_gather(part, axis), value)  161 us
  transfers between devices with their start and end apart: 16, of which 9 were waited for; matrix products, arithmetic and copies ran while one was open for 26% of the time, Pallas kernels for 0%

commit v1 on v0

v1 whole, which is shorter than its diff:
```python
import functools

import jax
import jax.numpy as jnp
from jax import lax
from jax.experimental import pallas as pl
from jax.experimental.pallas import tpu as pltpu
from jax.sharding import Mesh, PartitionSpec as P

EPS = 1e-05
INNER = 4096
MICRO = 2
CONV = 4352
F32 = jnp.float32
BF16 = jnp.bfloat16
AXES = ("rep", "x", "y", "z", "c")
SEQ = ("x", "y", "z", "c")
GROUPS = 8
TOK = 512
Q = 128
CH = TOK // Q

MESH = pl.DeviceIdType.MESH
ANY = pl.BlockSpec(memory_space=pl.ANY)
VM = pl.BlockSpec(memory_space=pltpu.VMEM)


class Net:
    def __init__(self, send, recv):
        self.send, self.recv, self.used, self.open = send, recv, 0, []
        self.keys = {}
        self.rep, self.x, self.y, self.z, self.c = (lax.axis_index(a) for a in AXES)
        self.ring = 2 * self.rep + self.y
        self.g = 2 * self.x + self.y
        self.m = 2 * self.z + self.c

    def at(self, dx=0, dy=0, dz=0, dc=0):
        ring = lax.rem(self.ring + dy, 4)
        return (ring // 2, lax.rem(self.x + dx, 4), lax.rem(ring, 2), lax.rem(self.z + dz, 4), lax.rem(self.c + dc, 2))

    def pair(self):
        return (self.rep, self.x, 1 - self.y, self.z, self.c)

    def group(self, d):
        g = lax.rem(self.g + d, 8)
        return (self.rep, g // 2, lax.rem(g, 2), self.z, self.c)

    def member(self, dz, dc):
        return 2 * lax.rem(self.z + dz, 4) + lax.rem(self.c + dc, 2)

    def push(self, src, dst, where):
        i = self.used
        self.used += 1
        copy = pltpu.make_async_remote_copy(
            src_ref=src, dst_ref=dst, send_sem=self.send.at[i], recv_sem=self.recv.at[i], device_id=where, device_id_type=MESH
        )
        copy.start()
        self.open.append(copy)
        return copy

    def copy(self, key, src, dst, where):
        i = self.keys.setdefault(key, len(self.keys))
        return pltpu.make_async_remote_copy(
            src_ref=src, dst_ref=dst, send_sem=self.send.at[i], recv_sem=self.recv.at[i], device_id=where, device_id_type=MESH
        )

    def behind(self, d):
        return 2 * lax.rem(self.x + 4 - d, 4) + self.y

    def local(self, src, dst):
        i = self.used
        self.used += 1
        copy = pltpu.make_async_copy(src, dst, self.recv.at[i])
        copy.start()
        return copy

    def meet(self, peers):
        barrier = pltpu.get_barrier_semaphore()
        for peer in peers:
            pl.semaphore_signal(barrier, inc=1, device_id=peer, device_id_type=MESH)
        pl.semaphore_wait(barrier, len(peers))

    def finish(self):
        for copy in self.open:
            copy.wait_send()


OTHERS = [(dz, dc) for dz in (0, 1, 3, 2) for dc in (0, 1) if (dz, dc) != (0, 0)]
ZS = (0, 1, 3, 2)
XS = (1, 3, 2)


def call(kernel, name, cid, outs, ins, spaces_in, spaces_out, sems, scratch=(), cost=1 << 20):
    return pl.pallas_call(
        kernel,
        name=name,
        out_shape=outs,
        in_specs=spaces_in,
        out_specs=spaces_out,
        scratch_shapes=[*scratch, pltpu.SemaphoreType.DMA((sems,)), pltpu.SemaphoreType.DMA((sems,))],
        compiler_params=pltpu.CompilerParams(collective_id=cid, has_side_effects=True, vmem_limit_bytes=60 << 20),
        cost_estimate=pl.CostEstimate(flops=0, bytes_accessed=cost, transcendentals=0),
    )(*ins)


def sds(shape, dtype):
    return jax.ShapeDtypeStruct(shape, dtype)


def gather_kernel(hid, wsend, small, hid_all, w_in, small_all, halo, send, recv):
    n = Net(send, recv)
    g, m, z, c, y = n.g, n.m, n.z, n.c, n.y
    n.meet(
        [n.at(dz=a, dc=b) for a, b in OTHERS] + [n.at(dx=d) for d in XS] + [n.at(dy=1), n.at(dy=3), n.group(1), n.group(7)]
    )
    own = [n.local(wsend.at[m], w_in.at[g, m]), n.local(small, small_all.at[g, m]), n.local(hid, hid_all.at[m])]
    w_cp, s_cp = {}, {}
    for a, b in OTHERS:
        w_cp[a, b] = n.push(wsend.at[n.member(a, b)], w_in.at[g, m], n.at(dz=a, dc=b))
        s_cp[a, b] = n.push(small, small_all.at[g, m], n.at(dz=a, dc=b))
    last = []

    def along_y(ref, group, pick):
        for half, dy in ((0, 1), (1, 3)):
            part = pick(ref, group, half)
            last.append(n.push(part, part, n.at(dy=dy)))

    def w_half(k):
        first = 2 * lax.rem(z + 4 - ZS[k], 4)
        return lambda ref, group, half: ref.at[group, pl.ds(first, 2), pl.ds(16 * half, 16)]

    x_cp = {}
    for cp in own:
        cp.wait()
    for k, a in enumerate(ZS):
        for b in (0, 1):
            if (a, b) != (0, 0):
                w_cp[a, b].wait_recv()
        block = w_in.at[g, pl.ds(2 * lax.rem(z + 4 - a, 4), 2)]
        for d in XS:
            x_cp[k, d] = n.push(block, block, n.at(dx=d))
        along_y(w_in, g, w_half(k))
    h_cp = {a: n.push(hid, hid_all.at[m], n.at(dz=a)) for a in (1, 3, 2)}
    h_sib = n.push(hid, hid_all.at[m], n.at(dc=1))
    for a, b in OTHERS:
        s_cp[a, b].wait_recv()
    s_x = {d: n.push(small_all.at[g], small_all.at[g], n.at(dx=d)) for d in XS}
    last.append(n.push(small_all.at[g], small_all.at[g], n.pair()))
    for d in XS:
        other = 2 * lax.rem(n.x + 4 - d, 4) + y
        for k in range(4):
            x_cp[k, d].wait_recv()
            along_y(w_in, other, w_half(k))
        s_x[d].wait_recv()
        last.append(n.push(small_all.at[other], small_all.at[other], n.pair()))
        h_cp[d].wait_recv()
        theirs = hid_all.at[2 * lax.rem(z + 4 - d, 4) + c]
        last.append(n.push(theirs, theirs, n.at(dc=1)))
    h_sib.wait_recv()
    for cp in last:
        cp.wait_recv()
    edge = n.push(hid_all.at[7, :, pl.ds(48, 16)], halo, n.group(1))
    edge.wait_recv()
    n.finish()


def gather(hid, wsend, small):
    outs = [sds((8, 2, 64, 2048), BF16), sds((8, 8, 32, 1408), BF16), sds((8, 8, 8, 128), F32), sds((2, 16, 2048), BF16)]
    return call(gather_kernel, "gather", 0, outs, (hid, wsend, small), [VM] * 3, [ANY] * 4, 112)


def states_out(n, block, everyone):
    n.local(block, everyone.at[n.g]).wait()
    own = everyone.at[n.g]
    ahead = {d: n.push(own, own, n.at(dx=d)) for d in XS}
    last = []

    def along_y(group):
        last.append(n.push(everyone.at[group], everyone.at[group], n.pair()))

    along_y(n.g)

    def rest():
        for d in XS:
            ahead[d].wait_recv()
            along_y(2 * lax.rem(n.x + 4 - d, 4) + n.y)
        for cp in last:
            cp.wait_recv()

    return rest


def sums_kernel(mine, everyone, send, recv):
    n = Net(send, recv)
    n.meet([n.at(dz=a, dc=b) for a, b in OTHERS])
    everyone[n.m] = mine[...]
    for a, b in OTHERS:
        n.push(mine, everyone.at[n.m], n.at(dz=a, dc=b))
    for cp in n.open:
        cp.wait_recv()
    n.finish()


def member_gather(mine, name, cid):
    return call(sums_kernel, name, cid, sds((8, *mine.shape), mine.dtype), (mine,), [VM], VM, 16)


def a2a_kernel(mine, edge, theirs, edge_next, send, recv):
    n = Net(send, recv)
    n.meet([n.at(dz=a, dc=b) for a, b in OTHERS] + [n.group(1), n.group(7)])
    theirs[n.m] = mine[n.m]
    for a, b in OTHERS:
        n.push(mine.at[n.member(a, b)], theirs.at[n.m], n.at(dz=a, dc=b))
    n.push(edge, edge_next, n.group(7))
    for cp in n.open:
        cp.wait_recv()
    n.finish()


def bc_swap(mine, edge):
    return call(a2a_kernel, "bc_swap", 3, [sds(mine.shape, mine.dtype), sds(edge.shape, edge.dtype)], (mine, edge), [VM] * 2, [VM] * 2, 16)


def edge_kernel(edge, edge_next, send, recv):
    n = Net(send, recv)
    n.meet([n.group(1), n.group(7)])
    n.push(edge, edge_next, n.group(7)).wait_recv()
    n.finish()


def edge_back(edge):
    return call(edge_kernel, "edge", 6, sds(edge.shape, edge.dtype), (edge,), [VM], VM, 2)


def tokens_begin(n, part, near):
    return [n.push(part.at[2 * lax.rem(n.z + d, 4) + 1 - n.c], near.at[d], n.at(dc=1)) for d in (1, 3, 2, 0)]


def tokens_middle(n, part, near, both, far, begun):
    away = []
    for cp, d in zip(begun, (1, 3, 2, 0)):
        cp.wait_recv()
        at = 2 * lax.rem(n.z + d, 4) + n.c
        for i in range(2):
            both[d, i] = (part[at, i].astype(F32) + near[d, i].astype(F32)).astype(BF16)
        if d:
            away.append(n.push(both.at[d], far.at[d - 1], n.at(dz=d)))
    return away


def tokens_end(both, far, out, away):
    for cp in away:
        cp.wait_recv()
    for i in range(2):
        out[i] = both[0, i].astype(F32) + far[0, i].astype(F32) + far[1, i].astype(F32) + far[2, i].astype(F32)


TOKEN_SCRATCH = [pltpu.VMEM((4, 2, 64, 2048), jnp.bfloat16), pltpu.VMEM((4, 2, 64, 2048), jnp.bfloat16), pltpu.VMEM((3, 2, 64, 2048), jnp.bfloat16)]


def backward_kernel(starts, part, starts_all, total, near, both, far, send, recv):
    n = Net(send, recv)
    n.meet([n.at(dz=a) for a in (1, 3, 2)] + [n.at(dc=1)] + [n.at(dx=d) for d in XS] + [n.pair()])
    rest = states_out(n, starts, starts_all)
    begun = tokens_begin(n, part, near)
    away = tokens_middle(n, part, near, both, far, begun)
    rest()
    tokens_end(both, far, total, away)
    n.finish()


def backward_states(starts, part):
    outs = [sds((8, *starts.shape), BF16), sds((2, 64, 2048), F32)]
    return call(backward_kernel, "states_backward", 4, outs, (starts, part), [VM, VM], [ANY, VM], 32, TOKEN_SCRATCH)


MA = 5


def add4(a, b):
    return a.astype(F32) + b[0].astype(F32) + b[1].astype(F32) + b[2].astype(F32)


def final_kernel(gw, go, part, small, gi, g_out, total, small_all, near, both, far, a1, a2, b1, b2, b3, pa, pb, oc, oa1, oa2, ob1, ob2, ob3, opa, opb, final, s1, s2, sx, sy, send, recv):
    n = Net(send, recv)
    x, y, z, c, rep, ring = n.x, n.y, n.z, n.c, n.rep, n.ring
    n.meet([n.at(dz=a, dc=b) for a, b in OTHERS] + [n.at(dx=d) for d in XS] + [n.at(dy=d) for d in XS])
    MB = 8 - MA

    swap = n.push(go.at[:, 1 - c], oc.at[pl.ds(4 * c, 4)], n.at(dc=1))
    for k in range(4):
        oc[4 * c + k] = go[k, c]
    begun = tokens_begin(n, part, near)
    A1 = {d: n.push(gw.at[pl.ds(2 * lax.rem(x + d, 4), 2), pl.ds(0, MA)], a1.at[d - 1], n.at(dx=d)) for d in XS}
    B1 = {}
    for d in XS:
        to = lax.rem(ring + d, 4)
        for k in range(4):
            B1[d, k] = n.push(gw.at[2 * k + lax.rem(to, 2), pl.ds(MA, MB), pl.ds(16 * (to // 2), 16)], b1.at[d - 1, k], n.at(dy=d))
    S1 = {d: n.push(small, s1.at[d - 1], n.at(dx=d)) for d in XS}
    away = tokens_middle(n, part, near, both, far, begun)
    swap.wait_recv()
    OA1 = {d: n.push(oc.at[pl.ds(2 * lax.rem(x + d, 4), 2), pl.ds(0, 32)], oa1.at[d - 1], n.at(dx=d)) for d in XS}
    OB1 = {}
    for d in XS:
        to = lax.rem(ring + d, 4)
        for k in range(4):
            OB1[d, k] = n.push(oc.at[2 * k + lax.rem(to, 2), pl.ds(32 + 16 * (to // 2), 16)], ob1.at[d - 1, k], n.at(dy=d))
    for d in XS:
        S1[d].wait_recv()
    sx[...] = small[...] + s1[0] + s1[1] + s1[2]
    S2 = {d: n.push(sx, s2.at[d - 1], n.at(dy=d)) for d in XS}
    for d in XS:
        for k in range(4):
            B1[d, k].wait_recv()
    for k in range(4):
        pb[k] = add4(gw[2 * k + y, pl.ds(MA, MB), pl.ds(16 * rep, 16)], b1[:, k]).astype(BF16)
    B2 = {d: n.push(pb.at[lax.rem(x + d, 4)], b2.at[d - 1], n.at(dx=d)) for d in XS}
    for d in XS:
        A1[d].wait_recv()
    for h in range(2):
        for k in range(MA):
            pa[h, k] = add4(gw[2 * x + h, k], a1[:, h, k]).astype(BF16)
    A2 = {d: n.push(pa.at[lax.rem(ring + d, 2)], a2.at[d - 1], n.at(dy=d)) for d in XS}
    for d in XS:
        for k in range(4):
            OB1[d, k].wait_recv()
    for k in range(4):
        opb[k] = add4(oc[2 * k + y, pl.ds(32 + 16 * rep, 16)], ob1[:, k]).astype(BF16)
    OB2 = {d: n.push(opb.at[lax.rem(x + d, 4)], ob2.at[d - 1], n.at(dx=d)) for d in XS}
    for d in XS:
        OA1[d].wait_recv()
    for h in range(2):
        opa[h] = add4(oc[2 * x + h, pl.ds(0, 32)], oa1[:, h]).astype(BF16)
    OA2 = {d: n.push(opa.at[lax.rem(ring + d, 2)], oa2.at[d - 1], n.at(dy=d)) for d in XS}
    for d in XS:
        S2[d].wait_recv()
    sy[...] = sx[...] + s2[0] + s2[1] + s2[2]
    small_all[n.m] = sy[...]
    S3 = [n.push(sy, small_all.at[n.m], n.at(dz=a, dc=b)) for a, b in OTHERS]
    for d in XS:
        B2[d].wait_recv()
    final[pl.ds(MA, MB), pl.ds(16 * rep, 16)] = add4(pb[x], b2).astype(BF16)
    mineb = final.at[pl.ds(MA, MB), pl.ds(16 * rep, 16)]
    B3 = n.push(mineb, mineb, n.at(dy=2))
    for d in XS:
        OB2[d].wait_recv()
    ob3[rep] = add4(opb[x], ob2)
    OB3 = n.push(ob3.at[rep], ob3.at[rep], n.at(dy=2))
    for d in XS:
        A2[d].wait_recv()
    for k in range(MA):
        final[k] = add4(pa[y, k], a2[:, k]).astype(BF16)
    B3.wait_recv()
    gi[n.m] = final[n.m]
    F = [n.push(final.at[n.member(a, b)], gi.at[n.m], n.at(dz=a, dc=b)) for a, b in OTHERS]
    for d in XS:
        OA2[d].wait_recv()
    g_out[pl.ds(0, 32)] = add4(opa[y], oa2)
    OB3.wait_recv()
    g_out[pl.ds(32, 16)] = ob3[0]
    g_out[pl.ds(48, 16)] = ob3[1]
    tokens_end(both, far, total, away)
    for cp in F + S3:
        cp.wait_recv()
    n.finish()


def final_exchange(gw, go, part, small):
    w = gw.shape[-1]
    MB = 8 - MA
    outs = [sds((8, 32, w), BF16), sds((64, 2048), F32), sds((2, 64, 2048), F32), sds((8, *small.shape), F32)]
    V = lambda *s: pltpu.VMEM(s, BF16)
    scratch = TOKEN_SCRATCH + [
        V(3, 2, MA, 32, w), V(3, MA, 32, w), V(3, 4, MB, 16, w), V(3, MB, 16, w), V(16, 128), V(2, MA, 32, w), V(4, MB, 16, w),
        V(8, 64, 2048), V(3, 2, 32, 2048), V(3, 32, 2048), V(3, 4, 16, 2048), V(3, 16, 2048), pltpu.VMEM((2, 16, 2048), F32), V(2, 32, 2048), V(4, 16, 2048),
        V(8, 32, w), pltpu.VMEM((3, *small.shape), F32), pltpu.VMEM((3, *small.shape), F32), pltpu.VMEM(small.shape, F32), pltpu.VMEM(small.shape, F32),
    ]
    return call(final_kernel, "gradients", 5, outs, (gw, go, part, small), [VM] * 4, [VM] * 4, 128, scratch)


NN = (((1,), (0,)), ((), ()))
NT = (((1,), (1,)), ((), ()))
TN = (((0,), (0,)), ((), ()))
TT = (((0,), (1,)), ((), ()))


def bdot(a, b, dims=NN):
    return lax.dot_general(a, b, dims, preferred_element_type=F32)


def parts(v, count):
    out = []
    for _ in range(count):
        p = v.astype(BF16)
        out.append(p)
        v = v - p.astype(F32)
    return out


def left_parts(v, w, count, dims=NN):
    return sum(bdot(p, w, dims) for p in parts(v, count))


def right_parts(w, v, count, dims=NN):
    return sum(bdot(w, p, dims) for p in parts(v, count))


def iota(shape, dim):
    return lax.broadcasted_iota(jnp.int32, shape, dim)


def spread_matrix():
    return (iota((128, 512), 0) == iota((128, 512), 1) // 64).astype(BF16)


def heads_of(v, eh):
    return left_parts(v, eh, 2)


def sums_of(v, eh):
    return left_parts(v, eh, 2, NT)


def lower_matrix():
    return (iota((Q, Q), 0) >= iota((Q, Q), 1)).astype(BF16)


def sigmoid(v):
    return 1.0 / (1.0 + jnp.exp(-v))


def softplus(v):
    return jnp.maximum(v, 0.0) + jnp.log1p(jnp.exp(-jnp.abs(v)))


def row_scale(h):
    return lax.rsqrt(jnp.mean(h * h, axis=-1, keepdims=True) + EPS)


def decays(L, flags):
    E = jnp.exp(L) * flags[:, 3:4]
    W = jnp.exp(L[Q - 1 : Q] - L) * flags[:, 4:5]
    return E, W


def wave_kernel(
    hid, halo, gain, w, conv, hp, flags, segrow, og, cot, outw, coef,
    normed, gate, pre, ext, delta, logs, mixed, carried, states, sums, dno, endlog, cot_all, w_out,
    proj_s, pre_s, gate_s, delta_s, logs_s, sloc, inner, dno_s, state, total, tail, ends, cot_s, w_o, w_s, send, recv, done,
):
    t = pl.program_id(0)
    c = lax.rem(t, CH)
    at = lax.rem(t, 8)
    micro = at // CH
    eh = spread_matrix()
    n = Net(send, recv)
    g, m, core = n.g, n.m, n.c

    def cot_z(a):
        return n.copy(("cot", a), cot_s.at[m], cot_s.at[m], n.at(dz=a))

    def cot_near():
        return n.copy("near", cot_s.at[m], cot_s.at[m], n.at(dc=1))

    def cot_on(a):
        theirs = cot_s.at[2 * lax.rem(n.z + 4 - a, 4) + core]
        return n.copy(("on", a), theirs, theirs, n.at(dc=1))

    def out_x(d):
        return n.copy(("ox", d), w_o.at[g], w_o.at[g], n.at(dx=d))

    def out_y(d, half):
        part = w_o.at[n.behind(d), pl.ds(32 * half, 32)]
        return n.copy(("oy", d, half), part, part, n.at(dy=3 if half else 1))

    def out_swap():
        return n.copy("swap", w_o.at[pl.ds(4 * (1 - core), 4)], w_s.at[:, core], n.at(dc=1))

    def end_x(i, d):
        return n.copy(("ex", i, d), ends.at[g, i], ends.at[g, i], n.at(dx=d))

    def end_y(i, d):
        part = ends.at[n.behind(d), i]
        return n.copy(("ey", i, d), part, part, n.pair())

    ALLX = (0,) + XS
    out_copies = [pltpu.make_async_copy(cot_s, cot_all, done.at[0]), pltpu.make_async_copy(w_s, w_out, done.at[1])]

    @pl.when(t == 0)
    def _():
        n.meet([n.at(dz=a) for a in (1, 3, 2)] + [n.at(dc=1)] + [n.at(dx=d) for d in XS] + [n.at(dy=1), n.at(dy=3)])
        cot_s[m] = cot[...]
        w_o[g] = outw[...]
        for d in XS:
            out_x(d).start()
        for half in (0, 1):
            out_y(0, half).start()
        for a in (1, 3, 2):
            cot_z(a).start()
        cot_near().start()

    @pl.when((t < 8) & (c == 0))
    def _():
        h = hid[...].reshape(TOK, 2048).astype(F32)
        nb = (h * row_scale(h) * gain[...]).astype(BF16)
        normed[...] = nb.reshape(8, 1, 64, 2048)
        e = halo[0].astype(F32)
        eb = (e * row_scale(e) * gain[...]).astype(BF16)
        proj_s[...] = bdot(jnp.concatenate([eb, nb], 0), w[...])
        tail[0:8] = proj_s[8:16, 512:1280].astype(BF16).astype(F32)
        state[...] = jnp.zeros_like(state)
        total[...] = jnp.zeros_like(total)

    @pl.when(t < 8)
    def _():
        rows = pl.ds(pl.multiple_of(16 + Q * c, 16), Q)
        f = flags[...]
        gt = proj_s[rows, 0:512]
        gate[...] = gt
        gate_s[at] = gt
        xbc = proj_s[rows, 512:1280].astype(BF16).astype(F32)
        tail[8:] = xbc
        acc = conv[4:5] + conv[3:4] * xbc
        for k in range(3):
            acc = acc + conv[k : k + 1] * tail[5 + k : 5 + k + Q] * f[:, k : k + 1]
        pre[...] = acc
        pre_s[at] = acc
        ext[0] = tail[...]
        d = softplus(proj_s[rows, 1280:1408] + hp[0:1])
        delta[...] = d
        delta_s[at] = d
        L = right_parts(lower_matrix(), d * hp[1:2], 3)
        logs[...] = L
        logs_s[at] = L
        E, W = decays(L, f)
        x = acc[:, :512]
        X = x * sigmoid(x)
        b = acc[:, 512:640]
        B = (b * sigmoid(b)).astype(BF16)
        S = right_parts(B, heads_of(W * d, eh) * X, 2, TN)
        sloc[at] = S
        both = heads_of(jnp.concatenate([E[Q - 8 :], L[Q - 8 :]], 0), eh)
        new = both[7:8] * state[...] + S
        state[...] = new
        tail[0:8] = tail[Q : Q + 8]
        lt = total[...] + L[Q - 1 : Q]
        total[...] = lt

        @pl.when(c == CH - 1)
        def _():
            ends[g, micro, 0:128] = new.astype(BF16)
            p = parts(jnp.broadcast_to(heads_of(jnp.broadcast_to(lt, (8, 128)), eh)[0:1], (16, 512)), 3)
            r = iota((16, 512), 0)
            ends[g, micro, 128:144] = jnp.where(r == 0, p[0], jnp.where(r == 1, p[1], jnp.where(r == 2, p[2], jnp.zeros_like(p[0]))))

    for i, when in ((0, CH - 1), (1, 2 * CH - 1)):

        @pl.when(t == when)
        def _(i=i):
            for d in XS:
                end_x(i, d).start()
            end_y(i, 0).start()

    @pl.when(t == 4)
    def _():
        for d in XS:
            out_x(d).wait_recv()
            for half in (0, 1):
                out_y(d, half).start()

    for i, when in ((0, 6), (1, 11)):

        @pl.when(t == when)
        def _(i=i):
            for d in XS:
                end_x(i, d).wait_recv()
                end_y(i, d).start()

    @pl.when(t == 8)
    def _():
        for d in ALLX:
            for half in (0, 1):
                out_y(d, half).wait_recv()
        out_swap().start()
        for k in range(4):
            w_s[k, core] = w_o[4 * core + k]
        for a in (1, 3, 2):
            cot_z(a).wait_recv()
            cot_on(a).start()

    @pl.when((t >= 8) & (t < 16))
    def _():
        L = logs_s[at]
        a = pre_s[at]
        X, B, C = activations(a)
        U = (heads_of(delta_s[at], eh) * X).astype(BF16)
        psi = bdot(C, B, NT)
        keep = same_mask(flags[...], segrow[0])
        LT = L.T
        for j in range(4):
            u = pair_halves(U[:, 128 * j : 128 * j + 128])
            y = jnp.zeros((Q, 128), F32)
            for e in range(2):
                h = 2 * j + e
                K = jnp.where(keep, jnp.exp(L[:, h : h + 1] - LT[h : h + 1]), 0.0)
                y = y + bdot((psi * K).astype(BF16), u[e])
            inner[at, :, 128 * j : 128 * j + 128] = y

    @pl.when(t == 16)
    def _():
        out_swap().wait_recv()
        cot_near().wait_recv()
        for a in (1, 3, 2):
            cot_on(a).wait_recv()
        for cp in out_copies:
            cp.start()
        for i in (0, 1):
            for d in ALLX:
                end_y(i, d).wait_recv()
        for q in range(8):
            for i in range(2):
                endlog[q, i] = ends[q, i, 128:144]

    @pl.when((t >= 16) & (c == 0))
    def _():
        dno_s[...] = bdot(cot_s[:, micro].reshape(TOK, 2048), w_s[...].reshape(512, 2048), NT)
        state[...] = entering(ends, coef, 0, micro)

    @pl.when(t >= 16)
    def _():
        f = flags[...]
        E, _ = decays(logs_s[at], f)
        a = pre_s[at]
        X, _, C = activations(a)
        more = heads_of(jnp.concatenate([E, jnp.broadcast_to(hp[2:3], (8, 128))], 0), eh)
        Ex, skip = more[:Q], more[Q : Q + 1]
        S = state[...]
        states[0, 0] = S
        Yc = Ex * bdot(C, S.astype(BF16))
        carried[...] = Yc
        mix = inner[at] + Yc + skip * X
        mixed[...] = mix
        after = Ex[Q - 1 : Q] * S + sloc[at]
        state[...] = after
        states[0, 1] = after
        gt = gate_s[at]
        gated = mix * (gt * sigmoid(gt))
        dn = dno_s[pl.ds(pl.multiple_of(Q * c, Q), Q)]
        dno[...] = dn
        ones = jnp.ones((8, 512), BF16)
        sums[0, 0:8] = right_parts(ones, gated * gated, 2, NT)
        sums[0, 8:16] = right_parts(ones, dn * og[...] * gated, 2, NT)

    @pl.when(t == 23)
    def _():
        for cp in out_copies:
            cp.wait()
        for a in (1, 3, 2):
            cot_z(a).wait_send()
            cot_on(a).wait_send()
        cot_near().wait_send()
        out_swap().wait_send()
        for d in XS:
            out_x(d).wait_send()
        for d in ALLX:
            for half in (0, 1):
                out_y(d, half).wait_send()
        for i in (0, 1):
            for d in XS:
                end_x(i, d).wait_send()
            for d in ALLX:
                end_y(i, d).wait_send()


def tile(width, at=lambda t: t):
    return pl.BlockSpec((Q, width), lambda t: (at(t), 0))


def whole(*shape):
    return pl.BlockSpec(shape, lambda t: (0,) * len(shape))


def plain(kernel, name, outs, ins, spaces_in, spaces_out, scratch=(), flops=1 << 30):
    return pl.pallas_call(
        kernel,
        name=name,
        grid=(MICRO * CH,),
        out_shape=outs,
        in_specs=spaces_in,
        out_specs=spaces_out,
        scratch_shapes=list(scratch),
        compiler_params=pltpu.CompilerParams(vmem_limit_bytes=56 << 20),
        cost_estimate=pl.CostEstimate(flops=flops, bytes_accessed=16 << 20, transcendentals=0),
    )(*ins)


T = MICRO * TOK
HID = pl.BlockSpec((2, 1, 64, 2048), lambda t: (t % CH, t // CH, 0, 0))


def agblock(width, at=lambda t: t):
    return pl.BlockSpec((2, 1, 64, width), lambda t: (at(t) % CH, at(t) // CH, 0, 0))


def wave(hid, halo, gain, w, conv, hp, flags, segrow, og, cot, outw, coef):
    outs = [
        sds((8, 2, 64, 2048), BF16), sds((T, 512), F32), sds((T, 768), F32), sds((8, Q + 8, 768), F32), sds((T, 128), F32), sds((T, 128), F32),
        sds((T, 512), F32), sds((T, 512), F32), sds((8, 2, 128, 512), F32), sds((8, 16, 128), F32), sds((T, 512), F32), sds((8, 2, 16, 512), BF16), sds((8, 2, 64, 2048), BF16), sds((4, 2, 64, 2048), BF16),
    ]
    first = lambda t: jnp.minimum(t, 7)
    last = lambda t: jnp.maximum(t - 16, 0)
    ring = lambda t: t % 8
    micro = pl.BlockSpec((8, 1, 64, 2048), lambda t: (0, first(t) // CH, 0, 0))
    V = lambda *shape: pltpu.VMEM(shape, F32)
    return pl.pallas_call(
        wave_kernel,
        name="wave",
        grid=(24,),
        out_shape=outs,
        in_specs=[
            micro, pl.BlockSpec((1, 16, 2048), lambda t: (first(t) // CH, 0, 0)), whole(1, 2048), whole(2048, 1408), whole(8, 768), whole(8, 128), tile(128, ring), blk(1, 128, ring), whole(1, 512),
            whole(2, 64, 2048), whole(64, 2048), SMEM,
        ],
        out_specs=[
            micro, tile(512, first), tile(768, first), blk(Q + 8, 768, first), tile(128, first), tile(128, first),
            tile(512, last), tile(512, last), pl.BlockSpec((1, 2, 128, 512), lambda t: (last(t), 0, 0, 0)), blk(16, 128, last), tile(512, last), whole(8, 2, 16, 512), ANY, ANY,
        ],
        scratch_shapes=[
            V(TOK + 16, 1408), V(8, Q, 768), V(8, Q, 512), V(8, Q, 128), V(8, Q, 128), V(8, 128, 512), V(8, Q, 512), V(TOK, 512), V(128, 512), V(1, 128), V(Q + 8, 768),
            pltpu.VMEM((8, 2, 144, 512), BF16), pltpu.VMEM((8, 2, 64, 2048), BF16), pltpu.VMEM((8, 64, 2048), BF16), pltpu.VMEM((4, 2, 64, 2048), BF16),
            pltpu.SemaphoreType.DMA((48,)), pltpu.SemaphoreType.DMA((48,)), pltpu.SemaphoreType.DMA((2,)),
        ],
        compiler_params=pltpu.CompilerParams(collective_id=1, has_side_effects=True, vmem_limit_bytes=60 << 20),
        cost_estimate=pl.CostEstimate(flops=8 << 30, bytes_accessed=32 << 20, transcendentals=0),
    )(hid, halo, gain, w, conv, hp, flags, segrow, og, cot, outw, coef)


def entering(everyone, coef, direction, micro, logs=None):
    total = jnp.zeros((128, 512), F32)
    at = 0 if everyone.shape[1] == 1 else micro
    rows = [(everyone[q, at, 128:144] if logs is None else logs[q, 0]).astype(F32) for q in range(8)]
    lt = [v[0:1] + v[1:2] + v[2:3] for v in rows]
    for q in range(8):
        log = sum(coef[80 * direction + 8 * q + r] * lt[r] for r in range(8))
        total = total + jnp.exp(log) * coef[80 * direction + 64 + 8 * micro + q] * everyone[q, at, 0:128].astype(F32)
    return total


def same_mask(flags, segrow):
    return (flags[:, 5:6] == segrow) & (iota((Q, Q), 0) >= iota((Q, Q), 1))


def activations(pre):
    a = pre * sigmoid(pre)
    return a[:, :512], a[:, 512:640].astype(BF16), a[:, 640:768].astype(BF16)


def pair_halves(v):
    low_half = iota(v.shape, 1) < 64
    zero = jnp.zeros_like(v)
    return jnp.where(low_half, v, zero), jnp.where(low_half, zero, v)


def blk(a, b, at=lambda t: t):
    return pl.BlockSpec((1, a, b), lambda t: (at(t), 0, 0))


SMEM = pl.BlockSpec(memory_space=pltpu.SMEM)


def column(row):
    return jnp.concatenate([jnp.broadcast_to(row, (128, 128)).T] * 4, 1)


def out_kernel(mixed, gate, dno, sums, pre, logs, flags, og, hp, nout, dmix, dgate, tloc, starts, small, state):
    t = pl.program_id(0)
    c = CH - 1 - lax.rem(t, CH)
    eh = spread_matrix()

    @pl.when(c == CH - 1)
    def _():
        state[...] = jnp.zeros_like(state)

    @pl.when(t == 0)
    def _():
        small[...] = jnp.zeros_like(small)

    tot = sums[0, 0]
    for q in range(1, 8):
        tot = tot + sums[q, 0]
    r = column(lax.rsqrt(tot[0:1] / INNER + EPS))
    s2 = column(tot[8:9] / INNER)
    gt = gate[...]
    s = sigmoid(gt)
    sg = gt * s
    mix = mixed[...]
    gated = mix * sg
    dn = dno[...]
    n0 = gated * r
    nout[...] = (n0 * og[...]).astype(BF16).reshape(2, 1, 64, 512)
    d_gated = r * (dn * og[...] - n0 * r * s2)
    dm = d_gated * sg
    dmix[...] = dm
    dgate[...] = (d_gated * mix * (s * (1.0 + gt * (1.0 - s)))).astype(BF16)
    x = pre[:, :512]
    X = x * sigmoid(x)
    cc = pre[:, 640:768]
    C = (cc * sigmoid(cc)).astype(BF16)
    small[0:1] += jnp.sum(dn * n0, 0, keepdims=True)
    small[1:2] += jnp.sum(X * dm, 0, keepdims=True)
    E, _ = decays(logs[...], flags[...])
    Ex = heads_of(E, eh)
    G = right_parts(C, Ex * dm, 2, TN)
    tloc[0] = G
    new = Ex[Q - 1 : Q] * state[...] + G
    state[...] = new

    @pl.when(c == 0)
    def _():
        starts[0] = new.astype(BF16)


def back_at(t):
    return (t // CH) * CH + (CH - 1 - t % CH)


def out_call(mixed, gate, dno, sums, pre, logs, flags, og, hp):
    outs = [sds((8, 2, 64, 512), BF16), sds((T, 512), F32), sds((T, 512), BF16), sds((8, 128, 512), F32), sds((2, 128, 512), BF16), sds((8, 512), F32)]
    b = back_at
    return plain(
        out_kernel, "out", outs, (mixed, gate, dno, sums, pre, logs, flags, og, hp),
        [tile(512, b), tile(512, b), tile(512, b), pl.BlockSpec((8, 1, 16, 128), lambda t: (0, back_at(t), 0, 0)), tile(768, b), tile(128, b), tile(128, b), whole(1, 512), whole(8, 128)],
        [agblock(512, b), tile(512, b), tile(512, b), blk(128, 512, b), blk(128, 512, lambda t: t // CH), whole(8, 512)],
        [pltpu.VMEM((128, 512), F32)],
    )


def back_kernel(pre, delta, logs, flags, segrow, mixed, carried, dmix, states, tloc, starts, ends, hp, coef, dpre, dbc, ddt, small, state):
    t = pl.program_id(0)
    c = CH - 1 - lax.rem(t, CH)
    eh = spread_matrix()

    @pl.when(c == CH - 1)
    def _():
        state[...] = entering(starts, coef, 1, t // CH, ends)

    @pl.when(t == 0)
    def _():
        small[...] = jnp.zeros_like(small)

    L = logs[...]
    f = flags[...]
    d = delta[...]
    E, W = decays(L, f)
    p = pre[...]
    s = sigmoid(p)
    X = p[:, :512] * s[:, :512]
    B = (p[:, 512:640] * s[:, 512:640]).astype(BF16)
    C = (p[:, 640:] * s[:, 640:]).astype(BF16)
    more = heads_of(jnp.concatenate([E, W, d, jnp.broadcast_to(hp[2:3], (8, 128))], 0), eh)
    Ex, Wx, dx, skip = more[:Q], more[Q : 2 * Q], more[2 * Q : 3 * Q], more[3 * Q : 3 * Q + 1]
    U = dx * X
    Ub = U.astype(BF16)
    dm = dmix[...]
    dmb = dm.astype(BF16)
    Yc = carried[...]
    Yi = mixed[...] - Yc - skip * X
    G = state[...]
    Gb = G.astype(BF16)
    psi = bdot(C, B, NT)
    keep = same_mask(f, segrow[0])
    LT = L.T
    dpsi = jnp.zeros((Q, Q), F32)
    cols = []
    for j in range(4):
        js = slice(128 * j, 128 * j + 128)
        u = pair_halves(Ub[:, js])
        y = pair_halves(dmb[:, js])
        acc = jnp.zeros((Q, 128), F32)
        for e in range(2):
            h = 2 * j + e
            K = jnp.where(keep, jnp.exp(L[:, h : h + 1] - LT[h : h + 1]), 0.0)
            acc = acc + bdot((psi * K).astype(BF16), y[e], TN)
            dpsi = dpsi + bdot(y[e], u[e], NT) * K
        cols.append(acc)
    dUi = jnp.concatenate(cols, 1)
    dUc = Wx * bdot(B, Gb)
    dU = dUi + dUc
    S0, S1 = states[0, 0], states[0, 1]
    dpb = dpsi.astype(BF16)
    dbc[0:128] = (bdot(C, dpb, TN) + bdot(Gb, (Wx * U).astype(BF16), NT)).astype(BF16)
    dbc[128:256] = (bdot(B, dpb, TT) + bdot(S0.astype(BF16), (Ex * dm).astype(BF16), NT)).astype(BF16)
    dL = sums_of(dmb.astype(F32) * Yi + dm * Yc - Ub.astype(F32) * dUi - U * dUc, eh)
    end = sums_of(jnp.broadcast_to(jnp.sum(G * S1, 0, keepdims=True), (8, 512)), eh)[0:1]
    upper = (iota((Q, Q), 0) <= iota((Q, Q), 1)).astype(BF16)
    dstep = right_parts(upper, dL, 3) + end
    rate = hp[1:2]
    dd = sums_of(dU * X, eh) + dstep * rate
    dr = dd * (1.0 - jnp.exp(-d))
    ddt[...] = dr.astype(BF16)
    small[0:1] += jnp.sum(dr, 0, keepdims=True)
    small[1:2] += jnp.sum(dstep * d * rate, 0, keepdims=True)
    sx = s[:, :512]
    dpre[...] = (dx * dU + skip * dm) * (sx * (1.0 + p[:, :512] * (1.0 - sx)))
    state[...] = Ex[Q - 1 : Q] * G + tloc[0]


def back_call(pre, delta, logs, flags, segrow, mixed, carried, dmix, states, tloc, starts, ends, hp, coef):
    outs = [sds((T, 512), F32), sds((256, T), BF16), sds((T, 128), BF16), sds((8, 128), F32)]
    b = back_at
    return plain(
        back_kernel, "back", outs, (pre, delta, logs, flags, segrow, mixed, carried, dmix, states, tloc, starts, ends, hp, coef),
        [tile(768, b), tile(128, b), tile(128, b), tile(128, b), blk(1, 128, b), tile(512, b), tile(512, b), tile(512, b), pl.BlockSpec((1, 2, 128, 512), lambda t: (back_at(t), 0, 0, 0)), blk(128, 512, b), pl.BlockSpec((8, 1, 128, 512), lambda t: (0, t // CH, 0, 0)), pl.BlockSpec((8, 1, 16, 512), lambda t: (0, t // CH, 0, 0)), whole(8, 128), SMEM],
        [tile(512, b), pl.BlockSpec((256, Q), lambda t: (0, back_at(t))), tile(128, b), whole(8, 128)],
        [pltpu.VMEM((128, 512), F32)],
    )


def pick_matrix(rows, start, count, shift, dtype=BF16):
    r, l = iota((rows, 128), 0), iota((rows, 128), 1)
    return ((r - start == l - shift) & (l >= shift) & (l < shift + count)).astype(dtype)


def bc_kernel(parts_in, pre, where, dpre):
    total = parts_in[0].astype(F32)
    for q in range(1, 8):
        total = total + parts_in[q].astype(F32)
    eye = pick_matrix(32, 0, 32, 0)
    d = left_parts(total, eye, 2, TN)
    p = left_parts(pre[:, 512:768], pick_matrix(256, 32 * where[0], 32, 0), 3)
    s = sigmoid(p)
    dpre[...] = d * (s * (1.0 + p * (1.0 - s)))


def bc_call(parts_in, pre, where):
    return plain(
        bc_kernel, "bc", sds((T, 128), F32), (parts_in, pre, where),
        [pl.BlockSpec((8, 32, Q), lambda t: (0, 0, t)), tile(768), SMEM], tile(128),
    )


def conv_back_kernel(dpre, dbc, nextx, nextbc, ext, flags, fnext, conv, ddt, dgate, where, w_b, hid, dproj, small, dn, gnorm, ahead, e, rows):
    t = pl.program_id(0)
    c = CH - 1 - lax.rem(t, CH)

    @pl.when(c == CH - 1)
    def _():
        ahead[Q:, 0:512] = nextx[0]
        ahead[Q:, 512:640] = nextbc[0]

    @pl.when(t == 0)
    def _():
        small[...] = jnp.zeros_like(small)

    pick = pick_matrix(256, 32 * where[0], 32, 0)
    ahead[0:Q, 0:512] = dpre[...]
    ahead[0:Q, 512:640] = dbc[...]
    dp = ahead[0:Q]
    cw = jnp.concatenate([conv[:, 0:512], left_parts(conv[:, 512:768], pick, 3)], 1)
    e[:, 0:512] = ext[0, :, 0:512]
    e[:, 512:640] = bdot(ext[0, :, 512:768].astype(BF16), pick)
    f, fn = flags[...], fnext[...]
    dx = cw[3:4] * dp
    small[3:4] += jnp.sum(dp * e[8 : 8 + Q], 0, keepdims=True)
    small[4:5] += jnp.sum(dp, 0, keepdims=True)
    for k in range(3):
        small[k : k + 1] += jnp.sum(dp * e[5 + k : 5 + k + Q] * f[:, k : k + 1], 0, keepdims=True)
        dx = dx + cw[k : k + 1] * ahead[3 - k : 3 - k + Q] * fn[:, k : k + 1]
    moved = bdot(ddt[...], pick_matrix(128, 0, 8, 32))
    full = jnp.concatenate([dgate[...], dx[:, 0:512].astype(BF16), (dx[:, 512:640] + moved).astype(BF16)], 1)
    dproj[...] = full.reshape(2, 1, 64, 1152)
    rows[pl.ds(pl.multiple_of(Q * c, Q), Q)] = full
    ahead[Q:] = ahead[0:8]

    @pl.when(c == 0)
    def _():
        d = bdot(rows[...], w_b[...], NT)
        dn[...] = d.astype(BF16).reshape(8, 1, 64, 2048)
        h = hid[...].reshape(TOK, 2048).astype(F32)
        part = jnp.sum(d * (h * row_scale(h)), 0, keepdims=True)

        @pl.when(t < CH)
        def _():
            gnorm[...] = part

        @pl.when(t >= CH)
        def _():
            gnorm[...] += part


def conv_back_call(dpre, dbc, nextx, nextbc, ext, flags, fnext, conv, ddt, dgate, where, w_b, hid):
    b = back_at
    micro = lambda t: t // CH
    return plain(
        conv_back_kernel, "conv_back", [sds((8, 2, 64, 1152), BF16), sds((8, 640), F32), sds((8, 2, 64, 2048), BF16), sds((1, 2048), F32)], (dpre, dbc, nextx, nextbc, ext, flags, fnext, conv, ddt, dgate, where, w_b, hid),
        [tile(512, b), tile(128, b), blk(8, 512, micro), blk(8, 128, micro), blk(Q + 8, 768, b), tile(128, b), tile(128, b), whole(8, 768), tile(128, b), tile(512, b), SMEM, whole(2048, 1152), pl.BlockSpec((8, 1, 64, 2048), lambda t: (0, t // CH, 0, 0))],
        [agblock(1152, b), whole(8, 640), pl.BlockSpec((8, 1, 64, 2048), lambda t: (0, t // CH, 0, 0)), whole(1, 2048)],
        [pltpu.VMEM((Q + 8, 640), F32)] * 2 + [pltpu.VMEM((TOK, 1152), BF16)],
    )


def strips(v, zi, ci):
    r = v.shape[0]
    return lax.dynamic_slice(v.reshape(r, 2, 4, 4, 128), (0, ci, 0, zi, 0), (r, 1, 4, 1, 128)).reshape(r, 512)


def from_members(v):
    r = v.shape[1]
    return v.reshape(4, 2, r, 4, 128).transpose(2, 1, 3, 0, 4).reshape(r, 4096)


def from_heads(v):
    r = v.shape[1]
    return v.reshape(4, 2, r, 4, 2).transpose(2, 1, 3, 0, 4).reshape(r, 64)


def from_rows(v):
    return v.transpose(1, 0, 2).reshape(v.shape[1], 256)


def to_members(v):
    r = v.shape[0]
    return v.reshape(r, 2, 4, 4, 128).transpose(3, 1, 0, 2, 4).reshape(8, r, 512)


def xdot(a, b, dims=NN):
    return lax.dot_general(a, b, dims, preferred_element_type=F32)


def per_device(layer_in, cotangent, segment_ids, norm_gain, in_weight, conv_weight, conv_bias, dt_bias, a_log, skip_gain, out_gain, out_weight):
    xi, yi, zi, ci = (lax.axis_index(a) for a in SEQ)
    g = 2 * xi + yi
    m = 2 * zi + ci
    where = m.astype(jnp.int32).reshape(1)
    pack = jnp.concatenate([segment_ids[:, 0].astype(F32).reshape(-1), norm_gain, conv_weight.reshape(-1), conv_bias, dt_bias, a_log, skip_gain, out_gain, jnp.zeros((1024 - 567,), F32)]).reshape(8, 128)
    bc = jnp.broadcast_to(in_weight[None, :, 8192:8448], (8, 32, 256))
    dt_w = in_weight[:, 8448:].reshape(32, 2, 4, 4, 2).transpose(3, 1, 0, 2, 4).reshape(8, 32, 8)
    w_send = jnp.concatenate([to_members(in_weight[:, :4096]), to_members(in_weight[:, 4096:8192]), bc, dt_w, jnp.zeros((8, 32, 120), BF16)], 2)
    hid_all, w_in, small_all, halo = gather(layer_in[:, 0], w_send, pack)
    w_in = w_in.reshape(2048, 1408)
    full = small_all.reshape(64, 1024)
    seg_full = full[:, :128].reshape(64, 2, 64).transpose(1, 0, 2).reshape(2, 4096)
    full = full[:, 128:]
    norm_full = full[:, :32].reshape(1, 2048)
    conv_full = full[:, 32:372].reshape(64, 5, 68).transpose(1, 0, 2).reshape(5, CONV)
    conv = jnp.concatenate([strips(conv_full[:, :INNER], zi, ci), conv_full[:, INNER:]], 1)
    conv = jnp.pad(conv, ((0, 3), (0, 0)))
    hv = lax.dynamic_slice(full[:, 372:439].reshape(2, 4, 4, 2, 67), (ci, 0, zi, 0, 0), (1, 4, 1, 2, 67)).reshape(8, 67)
    og = hv[:, 3:].reshape(1, 512)
    hp = jnp.pad(jnp.stack([hv[:, 0], -jnp.exp(hv[:, 1]), hv[:, 2]]), ((0, 5), (0, 120)))

    padded = jnp.concatenate([jnp.full((MICRO, 8), -1.0, F32), seg_full, jnp.full((MICRO, 8), -2.0, F32)], 1)
    near = lax.dynamic_slice(padded, (0, g * TOK), (MICRO, TOK + 16))
    own = near[:, 8 : 8 + TOK]
    chunked = own.reshape(MICRO, CH, Q)
    before = jnp.concatenate([near[:, 7:8], chunked[:, :-1, -1]], 1)[:, :, None]
    lanes = [(near[:, 5 + k : 5 + k + TOK] == own).astype(F32).reshape(T) for k in range(3)]
    lanes += [(chunked == before).astype(F32).reshape(T), (chunked == chunked[:, :, -1:]).astype(F32).reshape(T), own.reshape(T)]
    flags = jnp.pad(jnp.stack(lanes, 1), ((0, 0), (0, 122)))
    fnext = jnp.pad(jnp.stack([(near[:, 11 - k : 11 - k + TOK] == own).astype(F32).reshape(T) for k in range(3)], 1), ((0, 0), (0, 125)))
    segrow = own.reshape(8, 1, Q)
    lasts = seg_full.reshape(MICRO, GROUPS, TOK)[:, :, -1]
    idx = jnp.arange(GROUPS)
    q, r = idx[:, None], idx[None, :]
    last_before = jnp.sum(jnp.where(idx == g - 1, lasts, 0.0), 1, keepdims=True)
    last_own = jnp.sum(jnp.where(idx == g, lasts, 0.0), 1, keepdims=True)
    ok_before = (idx < g) & (lasts == last_before)
    ok_after = (idx > g) & (jnp.roll(lasts, 1, axis=1) == last_own)
    coef = jnp.concatenate([((r > q) & (r < g)).astype(F32), ok_before.astype(F32), ((r > g) & (r < q)).astype(F32), ok_after.astype(F32)], 0).reshape(160)

    normed, gate, pre, ext, delta, logs, mixed, carried, states, sums, dno, ends_all, cot, w_out = wave(hid_all, halo, norm_full, w_in, conv, hp, flags, segrow, og, cotangent[:, 0], out_weight, coef)
    sums_all = member_gather(sums, "norm_sums", 2)
    nout, dmix, dgate, tloc, starts, small_o = out_call(mixed, gate, dno, sums_all, pre, logs, flags, og, hp)
    nout = nout.reshape(T, 512)
    branch = xdot(nout, w_out.reshape(512, 2048)).astype(BF16).reshape(8, 2, 64, 2048)
    g_wout = xdot(nout, cot.reshape(T, 2048), TN).astype(BF16).reshape(4, 2, 64, 2048)
    starts_all, own_branch = backward_states(starts, branch)
    dpre, dbc, ddt, small_b = back_call(pre, delta, logs, flags, segrow, mixed, carried, dmix, states, tloc, starts_all, ends_all, hp, coef)
    bc_all, nextx = bc_swap(dbc.reshape(8, 32, T), dpre.reshape(MICRO, TOK, 512)[:, :8])
    dpre_bc = bc_call(bc_all, pre, where)
    nextbc = edge_back(dpre_bc.reshape(MICRO, TOK, 128)[:, :8])
    tail = xdot(w_in[:, 1024:1280], pick_matrix(256, 32 * m, 32, 0)) + xdot(w_in[:, 1280:1408], pick_matrix(128, 0, 8, 32))
    w_b = jnp.concatenate([w_in[:, :1024], tail.astype(BF16)], 1)
    dproj, small_c, d_normed, g_norm = conv_back_call(dpre, dpre_bc, nextx, nextbc, ext, flags, fnext, conv, ddt, dgate, where, w_b, hid_all)
    gw = xdot(normed.reshape(T, 2048), dproj.reshape(T, 1152), TN).astype(BF16).reshape(8, 8, 32, 1152)
    g_skip = small_o[1].reshape(8, 64).sum(1)
    heads_g = jnp.pad(jnp.concatenate([small_b[0, :8], small_b[1, :8], g_skip]), (0, 128 - 24))
    small = jnp.concatenate([g_norm[0], small_c[:5].reshape(-1), small_o[0], heads_g, jnp.zeros((256,), F32)]).reshape(48, 128)
    gi, g_out, own_dn, small_sum = final_exchange(gw, g_wout, d_normed, small)
    gi = gi.astype(F32)
    hid_o = layer_in[:, 0].astype(F32)
    layer_out = (hid_o + own_branch).astype(BF16)
    ro = row_scale(hid_o)
    dg = own_dn * norm_full
    d_hid = ro * dg - hid_o * (ro * ro * ro) * jnp.mean(dg * hid_o, -1, keepdims=True)
    grad_in = (cotangent[:, 0].astype(F32) + d_hid).astype(BF16)
    g_in = jnp.concatenate([from_members(gi[:, :, :512]), from_members(gi[:, :, 512:1024]), from_rows(gi[:, :, 1024:1056]), from_heads(gi[:, :, 1056:1064])], 1)
    at = 8 * g + m
    g_norm = lax.dynamic_slice(small_sum[:, :16].sum(0).reshape(64, 32), (at, 0), (1, 32)).reshape(32)
    conv_s = small_sum[:, 16:41].reshape(8, 5, 640)
    conv_s = jnp.concatenate([from_members(conv_s[:, :, :512]), from_rows(conv_s[:, :, 512:544])], 1)
    conv_s = lax.dynamic_slice(conv_s, (0, 68 * at), (5, 68))
    og_s = from_members(small_sum[:, 41:45].reshape(8, 1, 512))[0]
    og_s = lax.dynamic_slice(og_s, (64 * at,), (64,))
    hd_s = from_heads(small_sum[:, 45, :24].reshape(8, 3, 8))
    hd_s = lax.dynamic_slice(hd_s, (0, at), (3, 1))
    return (layer_out[:, None], grad_in[:, None], g_norm, g_in, conv_s[:4], conv_s[4], hd_s[0], hd_s[1], hd_s[2], og_s, g_out)


def solution(mesh):
    fine = Mesh(mesh.devices.reshape(2, 4, 2, 4, 2), AXES)
    tok = P(None, "rep", SEQ, None)
    return jax.shard_map(
        per_device,
        mesh=fine,
        in_specs=(tok, tok, P(None, "rep", SEQ), P(SEQ), P(SEQ, None), P(None, SEQ), P(SEQ), P(SEQ), P(SEQ), P(SEQ), P(SEQ), P(SEQ, None)),
        out_specs=(tok, tok, P(SEQ), P(SEQ, None), P(None, SEQ), P(SEQ), P(SEQ), P(SEQ), P(SEQ), P(SEQ), P(SEQ, None)),
        check_vma=False,
    )
```

time: 4900 us -> 404 us (0.08)
  waiting for transfers between devices: 2520 us -> 0 us
  other arithmetic: 943 us -> 12.3 us
  blocking collectives: 798 us -> 0 us
  Pallas kernels: 0 us -> 338 us
  local copies, waits for them, and re-layouts: 317 us -> 27.8 us
  matrix products: 248 us -> 21.6 us
    all_gather x6 -> x0, waiting for transfers between devices: 1920 us -> none  [the longest x4 1920 us: entering(): everything = jax.tree.map(lambda part: lax.all_gather(part, axis), value)]
    select_n x256 -> x0, other arithmetic: 891 us -> none  [hop(): return jax.tree.map(lambda a, b: jnp.where(reached, a, b), new, before)]
    unnamed x2 -> x0, blocking collectives: 547 us -> none
    reduce_scatter x2 -> x0, waiting for transfers between devices: 370 us -> none  [the longest x1 370 us: weight_terms(): lax.psum_scatter(jnp.einsum('tn,tj->nj', left, proj_grads, preferred_elem...]
    pallas_call x0 -> x11, Pallas kernels: none -> 338 us  [the longest x6 216 us: call(): pl.pallas_call(kernel, name=name, out_shape=outs, in_specs=spaces_in, out...]
    all_gather x3 -> x0, blocking collectives: 244 us -> none  [the longest x2 161 us: entering(): everything = jax.tree.map(lambda part: lax.all_gather(part, axis), value)]
    mul x260 -> x1, local copies, waits for them, and re-layouts: 243 us -> 0.07 us  [per_device(): dg = own_dn * norm_full]
    dot_general x34 -> x5, matrix products: 248 us -> 21.6 us  [xdot(): return lax.dot_general(a, b, dims, preferred_element_type=F32)]
  transfers between devices with their start and end apart: 16 -> 0, of which waited for: 9 -> 0; matrix products, arithmetic and copies ran while one was open for 26% -> 0% of each run, Pallas kernels for 0% -> 0%
where the time goes in v1:
time: 404 us; the launch traced here: 403 us
  Pallas kernels  338 us (84%)
  local copies, waits for them, and re-layouts  27.8 us (7%)
  matrix products  21.6 us (5%)
  other arithmetic  12.3 us (3%)
    pallas_call x6, Pallas kernels, call(): pl.pallas_call(kernel, name=name, out_shape=outs, in_specs=spaces_in, out...  216 us
    pallas_call x1, Pallas kernels, wave(): pl.pallas_call(wave_kernel, name='wave', grid=(24,), out_shape=outs, in_s...  67.9 us
    pallas_call x4, Pallas kernels, plain(): pl.pallas_call(kernel, name=name, grid=(MICRO * CH,), out_shape=outs, in_...  54.1 us
    dot_general x5, matrix products, xdot(): return lax.dot_general(a, b, dims, preferred_element_type=F32)  21.6 us

profile of v1, /device:TPU:1, one launch (start us, length us, event | category | flops | bytes accessed | tf_op | source)
XLA Modules:
  0.0 402.7 jit_solution(7844356820645701235)
XLA Ops:
  2.8 0.7 convert_reduce_fusion
  3.6 0.8 reshape.276
  4.4 1.4 concatenate.39
  5.7 0.7 slice.165
  6.6 0.7 slice.164
  7.4 1.1 fusion.31
  9.3 1.0 concatenate.38.wsend
  10.3 69.0 %gather.1 = (bf16[8,2,64,2048]{3,2,1,0:T(8,128)(2,1)}, bf16[8,8,32,1408]{3,2,1,0:T(8,128)(2,1)}, f32[8,8,8,128]{3,2,1,0:T(8,128)}, bf16[2,16,2048]{2,1,0:T(8,128)(2,1)}) custom-call(bf16[2,64,2048]{2,1,0:T(8,128)(2,1)} %bitcast.147, bf16[8,32,1408]{2,1,0:T(8,128)(2,1)} %concatenate.38.wsend, f32[8,128]{1,0:T(8,128)} %bitcast.186), custom_call_target="tpu_custom_call" | custom-call | bytes 1048576 | tf_op jit(solution)/shard_map/gather/pallas_call | solution.py:94
  79.3 1.0 copy.160
  80.4 0.7 reshape.279.gain
  82.7 0.6 reshape.291.segrow
  84.1 0.6 reshape.324.coef
  85.2 0.7 reshape.292.og
  85.9 0.6 select_maximum_fusion.1.hp
  87.2 0.6 select_maximum_fusion.conv
  87.9 0.8 pad_convert_fusion.fnext
  88.9 0.8 pad.24.flags
  89.8 1.7 fusion.8
  91.5 1.3 fusion
  92.8 2.6 slice.225
  95.5 2.7 pad_maximum_fusion.w_b
  98.2 67.9 %wave.1 = (bf16[8,2,64,2048]{3,2,1,0:T(8,128)(2,1)}, f32[1024,512]{1,0:T(8,128)}, f32[1024,768]{1,0:T(8,128)}, f32[8,136,768]{2,1,0:T(8,128)}, f32[1024,128]{1,0...) custom-call(bf16[8,2,64,2048]{3,2,1,0:T(8,128)(2,1)} %get-tuple-elem, ...), custom_call_target="tpu_custom_call" | custom-call | flops 8589934592 | bytes 33554432 | tf_op jit(solution)/shard_map/wave/pallas_call | solution.py:716
  166.1 13.8 %norm_sums.1.sums = f32[8,8,16,128]{3,2,1,0:T(8,128)} custom-call(f32[8,16,128]{2,1,0:T(8,128)} %get-tuple-element.58.mine), custom_call_target="tpu_custom_call" | custom-call | bytes 1048576 | tf_op jit(solution)/shard_map/norm_sums/pallas_call | solution.py:94
  179.9 10.9 %out.1 = (bf16[8,2,64,512]{3,2,1,0:T(8,128)(2,1)}, f32[1024,512]{1,0:T(8,128)}, bf16[1024,512]{1,0:T(8,128)(2,1)}, f32[8,128,512]{2,1,0:T(8,128)}, bf16[2,128,512]{2,1,0:T(8,128)(2,1)}, /*index=5*/f32[8,512]{1,0:T(8,128)}) custom-call(f32[1024,512]{1,0:T(8,128)} %get-tuple-element.55.mixed, f32[1024,512]{1,0:T(8,128)} %get-tuple-element.56.gate, ...), custom_call_target="tpu_custom_call" | custom-call | flops 1073741824 | bytes 16777216 | tf_op jit(solution)/shard_map/out/pallas_call | solution.py:685
  190.9 5.1 %bitcast_convert_fusion.1 = bf16[512,2048]{1,0:T(8,128)(2,1)} fusion(bf16[8,2,64,512]{3,2,1,0:T(8,128)(2,1)} %get-tuple-element.62, bf16[8,2,64,2048]{3,2,1,0:T(8,128)(2,1)S(1)} %copy-done.11), kind=kOutput, calls=%fused_computation.2 | convolution fusion | flops 2148532224 | bytes 7340032 | tf_op jit(solution)/shard_map/dot_general | solution.py:1028
  195.9 0.8 slice_reduce_fusion.5
  197.0 4.3 %convolution_convert_fusion = bf16[1024,2048]{1,0:T(8,128)(2,1)} fusion(bf16[1024,512]{1,0:T(8,128)(2,1)S(1)} %bitcast.203, bf16[512,2048]{1,0:T(8,128)(2,1)S(1)} %bitcast.204), kind=kOutput, calls=%fused_computation.3 | convolution fusion | flops 2149580800 | bytes 7340032 | tf_op jit(solution)/shard_map/dot_general | solution.py:1028
  201.3 33.3 %states_backward.1 = (bf16[8,2,128,512]{3,2,1,0:T(8,128)(2,1)}, f32[2,64,2048]{2,1,0:T(8,128)}) custom-call(bf16[2,128,512]{2,1,0:T(8,128)(2,1)} %get-tuple-element.61.starts, bf16[8,2,64,2048]{3,2,1,0:T(8,128)(2,1)} %bitcast.149), custom_call_target="tpu_custom_call" | custom-call | bytes 1048576 | tf_op jit(solution)/shard_map/states_backward/pallas_call | solution.py:94
  234.6 17.3 %back.1 = (f32[1024,512]{1,0:T(8,128)}, bf16[256,1024]{1,0:T(8,128)(2,1)}, bf16[1024,128]{1,0:T(8,128)(2,1)}, f32[8,128]{1,0:T(8,128)}) custom-call(f32[1024,768]{1,0:T(8,128)} %get-tuple-element.59.pre, f32[1024,128]{1,0:T(8,128)} %get-tuple-element.66.delta, f32[1024,128]{1,0:T(8,128)} %get-tuple-element.60.logs, f32[1024,128]{1,0:T(8,128)} %pad.24.flags, ...), custom_call_target="tpu_custom_call" | custom-call | flops 1073741824 | bytes 16777216 | tf_op jit(solution)/shard_map/back/pallas_call | solution.py:685
  251.8 0.8 slice_bitcast_fusion.4
  252.6 1.4 slice.223.edge
  254.0 12.7 %bc_swap.1 = (bf16[8,32,1024]{2,1,0:T(8,128)(2,1)}, f32[2,8,512]{2,1,0:T(8,128)}) custom-call(bf16[8,32,1024]{2,1,0:T(8,128)(2,1)} %bitcast.165, f32[2,8,512]{2,1,0:T(8,128)} %slice.223.edge), custom_call_target="tpu_custom_call" | custom-call | bytes 1048576 | tf_op jit(solution)/shard_map/bc_swap/pallas_call | solution.py:94
  266.6 6.7 %bc.1.dbc = f32[1024,128]{1,0:T(8,128)} custom-call(bf16[8,32,1024]{2,1,0:T(8,128)(2,1)} %get-tuple-element.75.parts_in, f32[1024,768]{1,0:T(8,128)} %get-tuple-element.59.pre, s32[1]{0:T(128)} %bitcast.24.where), custom_call_target="tpu_custom_call" | custom-call | flops 1073741824 | bytes 16777216 | tf_op jit(solution)/shard_map/bc/pallas_call | solution.py:685
  273.4 1.3 slice.224.edge
  274.7 4.2 %edge.1.nextbc = f32[2,8,128]{2,1,0:T(8,128)} custom-call(f32[2,8,128]{2,1,0:T(8,128)} %slice.224.edge), custom_call_target="tpu_custom_call" | custom-call | bytes 1048576 | tf_op jit(solution)/shard_map/edge/pallas_call | solution.py:94
  278.9 19.2 %conv_back.1 = (bf16[8,2,64,1152]{3,2,1,0:T(8,128)(2,1)}, f32[8,640]{1,0:T(8,128)}, bf16[8,2,64,2048]{3,2,1,0:T(8,128)(2,1)}, f32[1,2048]{1,0:T(1,128)}) custom-call(f32[1024,512]{1,0:T(8,128)} %get-tuple-element.73.dpre, f32[1024,128]{1,0:T(8,128)} %bc.1.dbc, f32[2,8,512]{2,1,0:T(8,128)} %get-tuple-element.76.nextx, f32[2,8,128]{2,1,0:T(8,128)} %edge.1.nextbc, ...), custom_call_target="tpu_custom_call" | custom-call | flops 1073741824 | bytes 16777216 | tf_op jit(solution)/shard_map/conv_back/pallas_call | solution.py:685
  298.1 9.2 %bitcast_convert_fusion = bf16[2048,1152]{1,0:T(8,128)(2,1)} fusion(bf16[8,2,64,2048]{3,2,1,0:T(8,128)(2,1)S(1)} %copy-done.12, bf16[8,2,64,1152]{3,2,1,0:T(8,128)(2,1)} %get-tuple-element.80), kind=kOutput, calls=%fused_computation | convolution fusion | flops 4834197504 | bytes 11272192 | tf_op jit(solution)/shard_map/dot_general | solution.py:1028
  307.4 0.6 copy-done.6
  308.0 82.7 %gradients.1 = (bf16[8,32,1152]{2,1,0:T(8,128)(2,1)}, f32[64,2048]{1,0:T(8,128)}, f32[2,64,2048]{2,1,0:T(8,128)}, f32[8,48,128]{2,1,0:T(8,128)}) custom-call(bf16[8,8,32,1152]{3,2,1,0:T(8,128)(2,1)} %bitcast.148, bf16[4,2,64,2048]{3,2,1,0:T(8,128)(2,1)} %bitcast.154, bf16[8,2,64,2048]{3,2,1,0:T(8,128)(2,1)} %get-tuple-element.82.part, f32[48,128]{1,0:T(8,128)} %bitcast.179), custom_call_target="tpu_custom_call" | custom-call | bytes 1048576 | tf_op jit(solution)/shard_map/gradients/pallas_call | solution.py:94
  390.8 1.6 fusion.2
  392.4 2.7 fusion.10
  395.3 0.6 dynamic_slice.27
  396.1 0.5 fusion.29
  396.9 0.5 fusion.32
  397.5 0.5 slice_bitcast_fusion.2
  398.1 0.6 slice.207
  400.9 1.1 pad_maximum_fusion.1
  401.9 0.8 copy.173
  (145 shorter events, 8.2 us)
Async XLA Ops:
  179.9 11.0 %copy-start.11 = (bf16[8,2,64,2048]{3,2,1,0:T(8,128)(2,1)S(1)}, bf16[8,2,64,2048]{3,2,1,0:T(8,128)(2,1)}, u32[]{:S(2)}) copy-start(bf16[8,2,64,2048]{3,2,1,0:T(8,128)(2,1)} %get-tuple-element.81) | copy-start | bytes 12582916
  190.8 6.1 %copy-start.9 = (bf16[8,2,64,512]{3,2,1,0:T(8,128)(2,1)S(1)}, bf16[8,2,64,512]{3,2,1,0:T(8,128)(2,1)}, u32[]{:S(2)}) copy-start(bf16[8,2,64,512]{3,2,1,0:T(8,128)(2,1)} %get-tuple-element.62) | copy-start | bytes 3145732
  190.8 6.1 %copy-start.10 = (bf16[4,2,64,2048]{3,2,1,0:T(8,128)(2,1)S(1)}, bf16[4,2,64,2048]{3,2,1,0:T(8,128)(2,1)}, u32[]{:S(2)}) copy-start(bf16[4,2,64,2048]{3,2,1,0:T(8,128)(2,1)} %get-tuple-element.63) | copy-start | bytes 6291460
  278.9 19.2 %copy-start.12 = (bf16[8,2,64,2048]{3,2,1,0:T(8,128)(2,1)S(1)}, bf16[8,2,64,2048]{3,2,1,0:T(8,128)(2,1)}, u32[]{:S(2)}) copy-start(bf16[8,2,64,2048]{3,2,1,0:T(8,128)(2,1)} %get-tuple-element.65) | copy-start | bytes 12582916
  298.1 9.2 %copy-start.7 = (f32[8,640]{1,0:T(8,128)S(1)}, f32[8,640]{1,0:T(8,128)}, u32[]{:S(2)}) copy-start(f32[8,640]{1,0:T(8,128)} %get-tuple-element.84) | copy-start | bytes 61444
  298.1 9.2 %copy-start.8 = (f32[1,2048]{1,0:T(1,128)S(1)}, f32[1,2048]{1,0:T(1,128)}, u32[]{:S(2)}) copy-start(f32[1,2048]{1,0:T(1,128)} %get-tuple-element.83) | copy-start | bytes 24580
  307.4 0.6 copy-start.6
  308.0 82.7 %copy-start.1 = (bf16[2,1,64,2048]{3,2,1,0:T(8,128)(2,1)S(1)}, bf16[2,1,64,2048]{3,2,1,0:T(8,128)(2,1)}, u32[]{:S(2)}) copy-start(bf16[2,1,64,2048]{3,2,1,0:T(8,128)(2,1)} %param.12) | copy-start | bytes 1572868
  308.0 84.3 %copy-start.2 = (f32[2,64,2048]{2,1,0:T(8,128)S(1)}, f32[2,64,2048]{2,1,0:T(8,128)}, u32[]{:S(2)}) copy-start(f32[2,64,2048]{2,1,0:T(8,128)} %get-tuple-element.64) | copy-start | bytes 3145732
  308.0 84.3 %copy-start.3 = (bf16[2,1,64,2048]{3,2,1,0:T(8,128)(2,1)S(1)}, bf16[2,1,64,2048]{3,2,1,0:T(8,128)(2,1)}, u32[]{:S(2)}) copy-start(bf16[2,1,64,2048]{3,2,1,0:T(8,128)(2,1)} %param.13) | copy-start | bytes 1572868
  390.7 4.4 %copy-start.5 = (f32[8,48,128]{2,1,0:T(8,128)S(1)}, f32[8,48,128]{2,1,0:T(8,128)}, u32[]{:S(2)}) copy-start(f32[8,48,128]{2,1,0:T(8,128)} %get-tuple-element.88) | copy-start | bytes 589828
  390.7 7.9 %copy-start = (bf16[8,32,1152]{2,1,0:T(8,128)(2,1)S(1)}, bf16[8,32,1152]{2,1,0:T(8,128)(2,1)}, u32[]{:S(2)}) copy-start(bf16[8,32,1152]{2,1,0:T(8,128)(2,1)} %get-tuple-element.89) | copy-start | bytes 1769476
  399.6 2.3 copy-start.4
